TPU v7x, 512 devices: a whole 4x8x8 slice. The times are simulated.
512 devices in a mesh: chan: 16 (over y, core), pix: 32 (over x, z).
Axes of the slice: x: 4, y: 8, z: 8, core: 2. Of those that a mesh axis runs over, the one named last changes fastest.
Arguments:
- cubes: float32 [2, 512, 262144], P(None, 'chan', 'pix'), may hold values from -4000 to 4000
- start_block: float32 [2, 512, 8], replicated, may hold values from -6 to 6
Outputs:
- spectrum: float32 [2, 2, 256, 262144], P(None, None, 'chan', 'pix')
All inputs are finite; a program needn't handle non-finite values.
Results may differ from a plain program's by a relative error of at most 0.0003.
Values sent between devices are 32-bit elements; how exact they have to be, the bound alone decides.
No kernel may reach another device: no remote copies, remote signals or barrier semaphores. Data moves between devices by JAX's collectives and lax.ppermute only.
A program may use at most 64 MiB of HBM per device.

v0:
```python
import jax
import jax.numpy as jnp
from jax import lax
from jax.sharding import PartitionSpec as P

ITERS = 2


HP = lax.Precision.HIGHEST


def orthonormal(grown):
    inner = jnp.einsum("sfm,sfn->smn", grown, grown, precision=HP)
    lower = jnp.linalg.cholesky(inner)
    return lax.linalg.triangular_solve(lower, grown, left_side=False, lower=True, transpose_a=True)


def tables(count, width):
    rows = jnp.arange(count, dtype=jnp.int32)[:, None]
    cols = jnp.arange(width, dtype=jnp.int32)[None, :]
    phase = (rows * cols % width).astype(jnp.float32) * (2.0 * jnp.pi / width)
    norm = 1.0 / jnp.sqrt(jnp.float32(width))
    return (jnp.cos(phase) * norm, jnp.sin(phase) * norm)


def body(cubes, start_block):
    local = lax.all_to_all(cubes, "chan", split_axis=2, concat_axis=1, tiled=True)
    width = local.shape[1]
    total = local.shape[2] * lax.axis_size("chan") * lax.axis_size("pix")
    partial_cov = jnp.einsum("sfp,sgp->sfg", local, local, precision=HP) / total
    cov = lax.psum(partial_cov, ("chan", "pix"))
    basis = start_block
    for step in range(ITERS):
        basis = orthonormal(jnp.einsum("sfg,sgm->sfm", cov, basis, precision=HP))
    weights = jnp.einsum("sfm,sfp->smp", basis, local, precision=HP)
    cleaned = local - jnp.einsum("sfm,smp->sfp", basis, weights, precision=HP)
    cosine, sine = tables(width // 2, width)
    real_part = jnp.einsum("kf,sfp->skp", cosine, cleaned, precision=HP)
    imag_part = -jnp.einsum("kf,sfp->skp", sine, cleaned, precision=HP)
    stacked = jnp.stack([real_part, imag_part])
    return lax.all_to_all(stacked, "chan", split_axis=2, concat_axis=3, tiled=True)


def solution(mesh):
    placed = (P(None, "chan", "pix"), P())
    return jax.shard_map(
        body, mesh=mesh, in_specs=placed, out_specs=P(None, None, "chan", "pix"), check_vma=False
    )
```

profile of v0, /device:TPU:1, one launch (start us, length us, event | category | flops | bytes accessed | tf_op | source)
XLA Modules:
  0.0 494.3 jit_solution(14376673353087758321)
XLA Ops:
  6.5 0.0 copy-start
  6.5 0.0 all-reduce.2.cloned.1.call-start
  6.5 10.3 %copy.47 = f32[2,32,8192]{1,0,2:T(2,128)} copy(f32[2,32,8192]{2,1,0:T(8,128)} %param.5) | data formatting | bytes 4194304 | tf_op args[0]
  16.8 10.3 %reshape.20 = f32[16,1,32768]{2,1,0:T(1,128)S(1)} reshape(f32[8192,2,32]{2,1,0:T(2,128)} %bitcast.75) | data formatting | bytes 4194304
  27.2 61.1 %all_to_all.36 = f32[16,1,32768]{2,1,0:T(1,128)} all-to-all(f32[16,1,32768]{2,1,0:T(1,128)S(1)} %reshape.20), channel_id=1, replica_groups=mesh['chan'=16,'pix'=32] {'chan'}, dimensions={0} | all-to-all | bytes 4194304 | tf_op jit(solution)/shard_map/all_to_all | solution.py:27
  88.2 0.5 broadcast.69
  88.7 7.3 %reduce.4 = f32[16,32768]{1,0:T(8,128)S(1)} reduce(f32[16,1,32768]{2,1,0:T(1,128)} %all_to_all.36, f32[]{:T(128)} %broadcast.69), dimensions={1}, to_apply=%all_to_all.26.reduce_sub_computation | reduce | bytes 4194308 | tf_op jit(solution)/shard_map/all_to_all | solution.py:27
  96.0 9.0 %reshape.21 = f32[8192,2,32]{2,1,0:T(2,128)} reshape(f32[16,32768]{1,0:T(8,128)S(1)} %reduce.4) | data formatting | bytes 4194304
  105.0 10.3 %copy.48 = f32[2,32,16,512]{3,1,2,0:T(8,128)S(1)} copy(f32[2,32,16,512]{1,0,3,2:T(2,128)} %bitcast.74) | data formatting | bytes 4194304 | tf_op jit(solution)/shard_map/all_to_all | solution.py:27
  115.4 4.9 convolution_multiply_fusion
  120.2 0.0 all-reduce.2.cloned.1.call-update
  120.3 278.0 %all-reduce.2.cloned.1.call-done = f32[2,512,512]{2,1,0:T(8,128)} async-done(((f32[2,512,512]{2,1,0:T(8,128)}), f32[2,512,512]{2,1,0:T(8,128)}) %all-reduce.2.cloned.1.call-update) | async-done | bytes 2097168 | tf_op jit(solution)/shard_map/psum | solution.py:31
  398.2 0.0 copy-done
  398.3 3.4 fusion.31
  401.7 0.2 fusion.32
  401.9 0.1 copy.49
  401.9 1.4 custom-call.8
  403.4 0.1 select_reduce_fusion.1
  403.5 0.1 compare_reduce_fusion.1
  403.6 0.1 select_bitcast_fusion.1
  403.6 1.3 custom-call.9
  404.9 0.2 convolution_bitcast_fusion.2
  405.1 3.4 fusion.33
  408.6 0.2 fusion.34
  408.8 0.1 copy.52
  408.9 1.4 custom-call.10
  410.3 0.1 select_reduce_fusion
  410.4 0.1 compare_reduce_fusion
  410.5 0.1 select_bitcast_fusion
  410.6 1.3 custom-call.11
  411.8 0.2 convolution_bitcast_fusion.1
  412.1 1.1 fusion.35
  413.2 1.8 convolution_subtract_fusion
  415.0 5.2 %convolution_bitcast_fusion = f32[1,2,256,512]{2,3,1,0:T(8,128)S(1)} fusion(f32[2,512,512]{2,1,0:T(8,128)S(1)} %convolution_subtract_fusion), kind=kOutput, calls=%fused_computation.5 | convolution fusion | flops 1612578816 | bytes 3145728 | tf_op jit(solution)/shard_map/kf,sfp->skp/dot_general | solution.py:38
  420.2 5.4 %fusion = f32[1,2,256,512]{2,3,1,0:T(8,128)S(1)} fusion(f32[2,512,512]{2,1,0:T(8,128)S(1)} %convolution_subtract_fusion), kind=kOutput, calls=%fused_computation.4 | convolution fusion | flops 1612840960 | bytes 3145728 | tf_op jit(solution)/shard_map/kf,sfp->skp/dot_general | solution.py:39
  425.6 0.1 pad_maximum_fusion
  425.8 2.3 copy.57
  428.1 57.1 %all_to_all.37 = f32[2,2,256,512]{3,1,0,2:T(2,128)S(1)} all-to-all(f32[2,2,256,512]{3,1,0,2:T(2,128)} %copy.57), channel_id=1, replica_groups=mesh['chan'=16,'pix'=32] {'chan'}, dimensions={2} | all-to-all | bytes 4194304 | tf_op jit(solution)/shard_map/all_to_all | solution.py:41
  485.3 0.7 copy.58
  485.9 1.5 copy.62
  (4 shorter events, 0.0 us)
Async XLA Ops:
  6.5 391.7 %copy-start = (f32[2,512,8]{1,2,0:T(8,128)S(1)}, f32[2,512,8]{1,2,0:T(8,128)}, u32[]{:S(2)}) copy-start(f32[2,512,8]{1,2,0:T(8,128)} %param.6) | copy-start | bytes 98308
  6.5 391.7 %all-reduce.2.cloned.1.call-start = ((), (), s32[]{:S(2)}) async-start(), calls=%async_computation.2 | async-start | bytes 4194304 | tf_op jit(solution)/shard_map/psum | solution.py:31
Sparse Core Ops, SparseCore 0:
  120.4 277.8 all-reduce.1
where the time goes:
time: 495 us; the launch traced here: 494 us
  waiting for transfers between devices  278 us (56%)
  blocking collectives  118 us (24%)
  local copies, waits for them, and re-layouts  45.2 us (9%)
  matrix products  26.1 us (5%)
  between operations  13.5 us (3%)
  other arithmetic  13.4 us (3%)
    psum x1, waiting for transfers between devices, body(): cov = lax.psum(partial_cov, ('chan', 'pix'))  278 us
    all_to_all x1, blocking collectives, body(): lax.all_to_all(cubes, 'chan', split_axis=2, concat_axis=1, tiled=True)  61.1 us
    all_to_all x1, blocking collectives, body(): lax.all_to_all(stacked, 'chan', split_axis=2, concat_axis=3, tiled=True)  57.1 us
    unnamed x5, local copies, waits for them, and re-layouts  29.6 us
    all_to_all x2, local copies, waits for them, and re-layouts, body(): lax.all_to_all(cubes, 'chan', split_axis=2, concat_axis=1, tiled=True)  10.9 us
  transfers between devices with their start and end apart: 1, of which 1 were waited for; matrix products, arithmetic and copies ran while one was open for 0% of the time, Pallas kernels for 0%

commit v1 on v0

v1 whole, which is shorter than its diff:
```python
import jax
import jax.numpy as jnp
import numpy as np
from jax import lax
from jax.experimental import pallas as pl
from jax.experimental.pallas import tpu as pltpu
from jax.sharding import PartitionSpec as P

ITERS = 2
LANES = 128
HP = lax.Precision.HIGHEST
VMEM = pl.BlockSpec(memory_space=pltpu.VMEM)
ANY = pl.BlockSpec(memory_space=pl.ANY)
PARAMS = pltpu.CompilerParams(vmem_limit_bytes=40 * 1024 * 1024)


def swap(value, axis):
    return lax.all_to_all(value, axis, split_axis=0, concat_axis=0, tiled=True)


def to_all(value, axis):
    count = lax.axis_size(axis)
    return swap(jnp.broadcast_to(value[None], (count,) + value.shape), axis)


def split_pixels(cubes, parts):
    species, chans, pixels = cubes.shape
    step = pixels // parts

    def kernel(src, dst, sems):
        copies = [
            pltpu.make_async_copy(src.at[:, :, pl.ds(j * step, step)], dst.at[j], sems.at[j])
            for j in range(parts)
        ]
        for copy in copies:
            copy.start()
        for copy in copies:
            copy.wait()

    return pl.pallas_call(
        kernel,
        out_shape=jax.ShapeDtypeStruct((parts, species, chans, step), cubes.dtype),
        in_specs=[ANY],
        out_specs=ANY,
        scratch_shapes=[pltpu.SemaphoreType.DMA((parts,))],
    )(cubes)


def join_pixels(blocks):
    parts, halves, species, waves, step = blocks.shape

    def kernel(src, dst, sems):
        copies = [
            pltpu.make_async_copy(src.at[j], dst.at[:, :, :, pl.ds(j * step, step)], sems.at[j])
            for j in range(parts)
        ]
        for copy in copies:
            copy.start()
        for copy in copies:
            copy.wait()

    return pl.pallas_call(
        kernel,
        out_shape=jax.ShapeDtypeStruct((halves, species, waves, parts * step), blocks.dtype),
        in_specs=[ANY],
        out_specs=ANY,
        scratch_shapes=[pltpu.SemaphoreType.DMA((parts,))],
    )(blocks)


def dot(a, b, dims=((1,), (0,)), precision=HP):
    return lax.dot_general(a, b, (dims, ((), ())), precision=precision, preferred_element_type=jnp.float32)


def cube_of(x_ref, s):
    parts, _, chans, pixels = x_ref.shape
    return x_ref[:, s].reshape(parts * chans, pixels)


def grow(rows, x, scale, out_ref, s):
    modes = rows.shape[0]
    weights = dot(rows, x) * scale
    grown = dot(weights, x, ((1,), (1,)))
    for c in range(grown.shape[1] // LANES):
        out_ref[s * modes : (s + 1) * modes, c, :] = grown[:, c * LANES : (c + 1) * LANES]


def grown_rows(g_ref, s, modes):
    return jnp.concatenate([g_ref[s * modes : (s + 1) * modes, c, :] for c in range(g_ref.shape[1])], axis=1)


def orthonormal(rows):
    modes = rows.shape[0]
    index = lax.broadcasted_iota(jnp.int32, (modes, 1), 0)
    for j in range(modes - 1):
        pivot = rows[j : j + 1]
        prods = jnp.sum(rows * pivot, axis=1, keepdims=True)
        ratio = jnp.where(index > j, prods / prods[j : j + 1], 0.0)
        rows = rows - ratio * pivot
    norms = jnp.sum(rows * rows, axis=1, keepdims=True)
    inverse = lax.rsqrt(norms)
    inverse = inverse * (1.5 - 0.5 * norms * inverse * inverse)
    return rows * inverse


def first_kernel(scale, x_ref, start_ref, out_ref):
    for s in range(x_ref.shape[1]):
        grow(start_ref[s], cube_of(x_ref, s), scale, out_ref, s)


def next_kernel(scale, modes, x_ref, g_ref, out_ref):
    for s in range(x_ref.shape[1]):
        rows = orthonormal(grown_rows(g_ref, s, modes))
        grow(rows, cube_of(x_ref, s), scale, out_ref, s)


def parts_of(value, count):
    parts = []
    for _ in range(count):
        part = value.astype(jnp.bfloat16)
        parts.append(part)
        value = value - part.astype(jnp.float32)
    return parts


def last_kernel(modes, x_ref, g_ref, table_ref, out_ref):
    for s in range(x_ref.shape[1]):
        x = cube_of(x_ref, s)
        rows = orthonormal(grown_rows(g_ref, s, modes))
        weights = dot(rows, x)
        cleaned = x - dot(rows, weights, ((0,), (0,)))
        high, low = parts_of(cleaned, 2)
        stacked = jnp.concatenate([high, low, high], axis=0)
        spectrum = dot(table_ref[...], stacked, precision=None)
        out_ref[:, :, s] = spectrum.reshape(out_ref.shape[0], out_ref.shape[1], out_ref.shape[3], out_ref.shape[4])


def tables(owners, waves, width):
    k = np.arange(waves)[:, None]
    f = np.arange(width)[None, :]
    phase = 2.0 * np.pi * (k * f % width) / width
    both = np.stack([np.cos(phase), -np.sin(phase)]) / np.sqrt(width)
    rows = both.reshape(2, owners, waves // owners, width).transpose(1, 0, 2, 3).reshape(2 * waves, width)
    rows = rows.astype(np.float32)
    high = rows.astype(jnp.bfloat16)
    low = (rows - high.astype(np.float32)).astype(jnp.bfloat16)
    return np.concatenate([high, high, low], axis=1)


def body(cubes, start_block):
    owners = lax.axis_size("chan")
    species, chans, pixels = cubes.shape
    width = chans * owners
    modes = start_block.shape[2]
    waves = width // 2
    step = pixels // owners
    scale = 1.0 / (pixels * lax.axis_size("pix"))

    share = jax.ShapeDtypeStruct((species * modes, width // LANES, LANES), jnp.float32)

    def summed(part):
        row = jnp.sum(swap(part, "chan"), axis=0)
        row = jnp.sum(to_all(row, "pix"), axis=0)
        return to_all(row, "chan")

    x = swap(split_pixels(cubes, owners), "chan")
    grown = pl.pallas_call(
        lambda *refs: first_kernel(scale, *refs),
        out_shape=share, in_specs=[VMEM, VMEM], out_specs=VMEM, compiler_params=PARAMS,
    )(x, jnp.swapaxes(start_block, 1, 2))
    grown = summed(grown)
    for _ in range(ITERS - 1):
        grown = pl.pallas_call(
            lambda *refs: next_kernel(scale, modes, *refs),
            out_shape=share, in_specs=[VMEM, VMEM], out_specs=VMEM, compiler_params=PARAMS,
        )(x, grown)
        grown = summed(grown)
    blocks = pl.pallas_call(
        lambda *refs: last_kernel(modes, *refs),
        out_shape=jax.ShapeDtypeStruct((owners, 2, species, waves // owners, step), jnp.float32),
        in_specs=[VMEM, VMEM, VMEM], out_specs=VMEM, compiler_params=PARAMS,
    )(x, grown, jnp.asarray(tables(owners, waves, width)))
    return join_pixels(swap(blocks, "chan"))


def solution(mesh):
    placed = (P(None, "chan", "pix"), P())
    return jax.shard_map(
        body, mesh=mesh, in_specs=placed, out_specs=P(None, None, "chan", "pix"), check_vma=False
    )
```

time: 495 us -> 335 us (0.68)
  waiting for transfers between devices: 278 us -> 0 us
  Pallas kernels: 0 us -> 141 us
  blocking collectives: 118 us -> 191 us
  local copies, waits for them, and re-layouts: 45.2 us -> 1.46 us
  matrix products: 26.1 us -> 0 us
  between operations: 13.5 us -> 0.05 us
  other arithmetic: 13.4 us -> 0.14 us
    psum x1 -> x0, waiting for transfers between devices: 278 us -> none  [body(): cov = lax.psum(partial_cov, ('chan', 'pix'))]
    pallas_call x0 -> x5, Pallas kernels: none -> 141 us  [the longest x1 64.8 us: join_pixels(): pl.pallas_call(kernel, out_shape=jax.ShapeDtypeStruct((halves, species, w...]
    all_to_all x2 -> x8, blocking collectives: 118 us -> 191 us  [swap(): return lax.all_to_all(value, axis, split_axis=0, concat_axis=0, tiled=True)]
    unnamed x5 -> x4, local copies, waits for them, and re-layouts: 29.6 us -> 1.41 us
    dot_general x9 -> x0, matrix products: 25.7 us -> none  [the longest x2 6.87 us: body(): basis = orthonormal(jnp.einsum('sfg,sgm->sfm', cov, basis, precision=HP))]
    all_to_all x4 -> x0, local copies, waits for them, and re-layouts: 13.1 us -> none  [the longest x2 10.9 us: body(): lax.all_to_all(cubes, 'chan', split_axis=2, concat_axis=1, tiled=True)]
    all_to_all x1 -> x0, other arithmetic: 7.29 us -> none  [body(): lax.all_to_all(cubes, 'chan', split_axis=2, concat_axis=1, tiled=True)]
    another operation x13 -> x0, other arithmetic: 6.05 us -> none  [the longest x7 3.25 us: orthonormal(): lower = jnp.linalg.cholesky(inner)]
  transfers between devices with their start and end apart: 1 -> 0, of which waited for: 1 -> 0; matrix products, arithmetic and copies ran while one was open for 0% -> 0% of each run, Pallas kernels for 0% -> 0%
where the time goes in v1:
time: 335 us; the launch traced here: 334 us
  blocking collectives  191 us (57%)
  Pallas kernels  141 us (42%)
    all_to_all x8, blocking collectives, swap(): return lax.all_to_all(value, axis, split_axis=0, concat_axis=0, tiled=True)  191 us
    pallas_call x1, Pallas kernels, join_pixels(): pl.pallas_call(kernel, out_shape=jax.ShapeDtypeStruct((halves, species, w...  64.8 us
    pallas_call x1, Pallas kernels, split_pixels(): pl.pallas_call(kernel, out_shape=jax.ShapeDtypeStruct((parts, species, ch...  64.8 us

profile of v1, /device:TPU:1, one launch (start us, length us, event | category | flops | bytes accessed | tf_op | source)
XLA Modules:
  0.0 334.2 jit_solution(17298535135412805791)
XLA Ops:
  0.0 64.8 %shard_map.37 = f32[16,2,32,512]{3,2,1,0:T(8,128)} custom-call(f32[2,32,8192]{2,1,0:T(8,128)} %src.1), custom_call_target="tpu_custom_call" | custom-call | tf_op jit(solution)/shard_map/pallas_call | solution.py:40
  64.8 0.0 copy-start.1
  64.8 61.4 %all_to_all.40.refs_0_ = f32[16,2,32,512]{3,2,1,0:T(8,128)S(1)} all-to-all(f32[16,2,32,512]{3,2,1,0:T(8,128)} %shard_map.37), channel_id=1, replica_groups=mesh['chan'=16,'pix'=32] {'chan'}, dimensions={0} | all-to-all | bytes 4194304 | tf_op jit(solution)/shard_map/all_to_all | solution.py:18
  126.2 0.0 copy-done.1
  126.2 2.9 shard_map.38
  129.1 10.1 %all_to_all.41 = f32[16,4,128]{2,1,0:T(4,128)S(1)} all-to-all(f32[16,4,128]{2,1,0:T(4,128)S(1)} %shard_map.38), channel_id=1, replica_groups=mesh['chan'=16,'pix'=32] {'chan'}, dimensions={0} | all-to-all | bytes 65536 | tf_op jit(solution)/shard_map/all_to_all | solution.py:18
  139.3 19.7 %all_to_all.42 = f32[32,4,128]{2,1,0:T(4,128)S(1)} all-to-all(f32[32,4,128]{2,1,0:T(4,128)S(1)} %broadcast_in_dim.8), channel_id=1, replica_groups=mesh['chan'=16,'pix'=32] {'pix'}, dimensions={0} | all-to-all | bytes 131072 | tf_op jit(solution)/shard_map/all_to_all | solution.py:18
  159.1 11.7 %all_to_all.43.refs_1_ = f32[16,4,128]{2,1,0:T(4,128)S(1)} all-to-all(f32[16,4,128]{2,1,0:T(4,128)S(1)} %broadcast_in_dim.9), channel_id=1, replica_groups=mesh['chan'=16,'pix'=32] {'chan'}, dimensions={0} | all-to-all | bytes 65536 | tf_op jit(solution)/shard_map/all_to_all | solution.py:18
  170.8 3.5 %shard_map.39 = f32[16,4,128]{2,1,0:T(4,128)S(1)} custom-call(f32[16,2,32,512]{3,2,1,0:T(8,128)S(1)} %all_to_all.40.refs_0_, f32[16,4,128]{2,1,0:T(4,128)S(1)} %all_to_all.43.refs_1_), custom_call_target="tpu_custom_call" | custom-call | tf_op jit(solution)/shard_map/pallas_call | solution.py:173
  174.3 10.3 %all_to_all.44 = f32[16,4,128]{2,1,0:T(4,128)S(1)} all-to-all(f32[16,4,128]{2,1,0:T(4,128)S(1)} %shard_map.39), channel_id=1, replica_groups=mesh['chan'=16,'pix'=32] {'chan'}, dimensions={0} | all-to-all | bytes 65536 | tf_op jit(solution)/shard_map/all_to_all | solution.py:18
  184.6 11.9 %all_to_all.45 = f32[32,4,128]{2,1,0:T(4,128)S(1)} all-to-all(f32[32,4,128]{2,1,0:T(4,128)S(1)} %broadcast_in_dim.10), channel_id=1, replica_groups=mesh['chan'=16,'pix'=32] {'pix'}, dimensions={0} | all-to-all | bytes 131072 | tf_op jit(solution)/shard_map/all_to_all | solution.py:18
  196.5 11.5 %all_to_all.46.refs_1_ = f32[16,4,128]{2,1,0:T(4,128)S(1)} all-to-all(f32[16,4,128]{2,1,0:T(4,128)S(1)} %broadcast_in_dim.11), channel_id=1, replica_groups=mesh['chan'=16,'pix'=32] {'chan'}, dimensions={0} | all-to-all | bytes 65536 | tf_op jit(solution)/shard_map/all_to_all | solution.py:18
  208.1 0.0 copy-start
  208.1 1.4 copy-done
  209.5 5.4 %shard_map.40 = f32[16,2,2,16,512]{4,3,2,1,0:T(8,128)S(1)} custom-call(f32[16,2,32,512]{3,2,1,0:T(8,128)S(1)} %all_to_all.40.refs_0_, f32[16,4,128]{2,1,0:T(4,128)S(1)} %all_to_all.46.refs_1_, bf16[512,1536]{1,0:T(8,128)(2,1)S(1)} %copy-done), custom_call_target="tpu_custom_call" | custom-call | tf_op jit(solution)/shard_map/pallas_call | solution.py:178
  214.8 54.6 %all_to_all.47.src = f32[16,2,2,16,512]{4,3,2,1,0:T(8,128)} all-to-all(f32[16,2,2,16,512]{4,3,2,1,0:T(8,128)S(1)} %shard_map.40), channel_id=1, replica_groups=mesh['chan'=16,'pix'=32] {'chan'}, dimensions={0} | all-to-all | bytes 4194304 | tf_op jit(solution)/shard_map/all_to_all | solution.py:18
  269.4 64.8 %shard_map.41 = f32[2,2,16,8192]{3,2,1,0:T(8,128)} custom-call(f32[16,2,2,16,512]{4,3,2,1,0:T(8,128)} %all_to_all.47.src), custom_call_target="tpu_custom_call" | custom-call | tf_op jit(solution)/shard_map/pallas_call | solution.py:62
  (8 shorter events, 0.2 us)
Async XLA Ops:
  64.8 61.4 %copy-start.1 = (f32[2,512,8]{1,2,0:T(8,128)S(1)}, f32[2,512,8]{1,2,0:T(8,128)}, u32[]{:S(2)}) copy-start(f32[2,512,8]{1,2,0:T(8,128)} %param.4) | copy-start | bytes 98308
  208.1 1.4 copy-start

commit v2 on v1

--- a/solution.py
+++ b/solution.py
@@ -41,7 +41,7 @@
         kernel,
         out_shape=jax.ShapeDtypeStruct((parts, species, chans, step), cubes.dtype),
         in_specs=[ANY],
-        out_specs=ANY,
+        out_specs=VMEM,
         scratch_shapes=[pltpu.SemaphoreType.DMA((parts,))],
     )(cubes)
 
@@ -62,7 +62,7 @@
     return pl.pallas_call(
         kernel,
         out_shape=jax.ShapeDtypeStruct((halves, species, waves, parts * step), blocks.dtype),
-        in_specs=[ANY],
+        in_specs=[VMEM],
         out_specs=ANY,
         scratch_shapes=[pltpu.SemaphoreType.DMA((parts,))],
     )(blocks)

time: 335 us -> 211 us (0.63)
  Pallas kernels: 141 us -> 17.9 us
    pallas_call x1, Pallas kernels: 64.8 us -> 3.03 us  [join_pixels(): pl.pallas_call(kernel, out_shape=jax.ShapeDtypeStruct((halves, species, w...]
    pallas_call x1, Pallas kernels: 64.8 us -> 3.06 us  [split_pixels(): pl.pallas_call(kernel, out_shape=jax.ShapeDtypeStruct((parts, species, ch...]
where the time goes in v2:
time: 211 us
  blocking collectives  191 us (91%)
  Pallas kernels  17.9 us (8%)
    all_to_all x8, blocking collectives, swap(): return lax.all_to_all(value, axis, split_axis=0, concat_axis=0, tiled=True)  191 us
    pallas_call x1, Pallas kernels, body(): pl.pallas_call(lambda *refs: last_kernel(modes, *refs), out_shape=jax.Sha...  5.37 us

profile of v2, /device:TPU:1, one launch (start us, length us, event | category | flops | bytes accessed | tf_op | source)
XLA Modules:
  0.0 210.7 jit_solution(3134002635778442216)
XLA Ops:
  0.0 3.1 %shard_map.37 = f32[16,2,32,512]{3,2,1,0:T(8,128)} custom-call(f32[2,32,8192]{2,1,0:T(8,128)} %src.1), custom_call_target="tpu_custom_call" | custom-call | tf_op jit(solution)/shard_map/pallas_call | solution.py:40
  3.1 0.0 copy-start.1
  3.1 61.4 %all_to_all.40.refs_0_ = f32[16,2,32,512]{3,2,1,0:T(8,128)S(1)} all-to-all(f32[16,2,32,512]{3,2,1,0:T(8,128)} %shard_map.37), channel_id=1, replica_groups=mesh['chan'=16,'pix'=32] {'chan'}, dimensions={0} | all-to-all | bytes 4194304 | tf_op jit(solution)/shard_map/all_to_all | solution.py:18
  64.5 0.0 copy-done.1
  64.5 2.9 %shard_map.38 = f32[16,4,128]{2,1,0:T(4,128)S(1)} custom-call(f32[16,2,32,512]{3,2,1,0:T(8,128)S(1)} %all_to_all.40.refs_0_, f32[2,8,512]{2,1,0:T(8,128)S(1)} %bitcast.1), custom_call_target="tpu_custom_call" | custom-call | tf_op jit(solution)/shard_map/pallas_call | solution.py:167
  67.4 10.1 %all_to_all.41 = f32[16,4,128]{2,1,0:T(4,128)S(1)} all-to-all(f32[16,4,128]{2,1,0:T(4,128)S(1)} %shard_map.38), channel_id=1, replica_groups=mesh['chan'=16,'pix'=32] {'chan'}, dimensions={0} | all-to-all | bytes 65536 | tf_op jit(solution)/shard_map/all_to_all | solution.py:18
  77.5 19.7 %all_to_all.42 = f32[32,4,128]{2,1,0:T(4,128)S(1)} all-to-all(f32[32,4,128]{2,1,0:T(4,128)S(1)} %broadcast_in_dim.8), channel_id=1, replica_groups=mesh['chan'=16,'pix'=32] {'pix'}, dimensions={0} | all-to-all | bytes 131072 | tf_op jit(solution)/shard_map/all_to_all | solution.py:18
  97.3 11.7 %all_to_all.43.refs_1_ = f32[16,4,128]{2,1,0:T(4,128)S(1)} all-to-all(f32[16,4,128]{2,1,0:T(4,128)S(1)} %broadcast_in_dim.9), channel_id=1, replica_groups=mesh['chan'=16,'pix'=32] {'chan'}, dimensions={0} | all-to-all | bytes 65536 | tf_op jit(solution)/shard_map/all_to_all | solution.py:18
  109.0 3.5 %shard_map.39 = f32[16,4,128]{2,1,0:T(4,128)S(1)} custom-call(f32[16,2,32,512]{3,2,1,0:T(8,128)S(1)} %all_to_all.40.refs_0_, f32[16,4,128]{2,1,0:T(4,128)S(1)} %all_to_all.43.refs_1_), custom_call_target="tpu_custom_call" | custom-call | tf_op jit(solution)/shard_map/pallas_call | solution.py:173
  112.6 10.3 %all_to_all.44 = f32[16,4,128]{2,1,0:T(4,128)S(1)} all-to-all(f32[16,4,128]{2,1,0:T(4,128)S(1)} %shard_map.39), channel_id=1, replica_groups=mesh['chan'=16,'pix'=32] {'chan'}, dimensions={0} | all-to-all | bytes 65536 | tf_op jit(solution)/shard_map/all_to_all | solution.py:18
  122.9 11.9 %all_to_all.45 = f32[32,4,128]{2,1,0:T(4,128)S(1)} all-to-all(f32[32,4,128]{2,1,0:T(4,128)S(1)} %broadcast_in_dim.10), channel_id=1, replica_groups=mesh['chan'=16,'pix'=32] {'pix'}, dimensions={0} | all-to-all | bytes 131072 | tf_op jit(solution)/shard_map/all_to_all | solution.py:18
  134.8 11.5 %all_to_all.46.refs_1_ = f32[16,4,128]{2,1,0:T(4,128)S(1)} all-to-all(f32[16,4,128]{2,1,0:T(4,128)S(1)} %broadcast_in_dim.11), channel_id=1, replica_groups=mesh['chan'=16,'pix'=32] {'chan'}, dimensions={0} | all-to-all | bytes 65536 | tf_op jit(solution)/shard_map/all_to_all | solution.py:18
  146.3 0.0 copy-start
  146.3 1.4 copy-done
  147.8 5.4 %shard_map.40 = f32[16,2,2,16,512]{4,3,2,1,0:T(8,128)S(1)} custom-call(f32[16,2,32,512]{3,2,1,0:T(8,128)S(1)} %all_to_all.40.refs_0_, f32[16,4,128]{2,1,0:T(4,128)S(1)} %all_to_all.46.refs_1_, bf16[512,1536]{1,0:T(8,128)(2,1)S(1)} %copy-done), custom_call_target="tpu_custom_call" | custom-call | tf_op jit(solution)/shard_map/pallas_call | solution.py:178
  153.1 54.6 %all_to_all.47.src = f32[16,2,2,16,512]{4,3,2,1,0:T(8,128)} all-to-all(f32[16,2,2,16,512]{4,3,2,1,0:T(8,128)S(1)} %shard_map.40), channel_id=1, replica_groups=mesh['chan'=16,'pix'=32] {'chan'}, dimensions={0} | all-to-all | bytes 4194304 | tf_op jit(solution)/shard_map/all_to_all | solution.py:18
  207.7 3.0 %shard_map.41 = f32[2,2,16,8192]{3,2,1,0:T(8,128)} custom-call(f32[16,2,2,16,512]{4,3,2,1,0:T(8,128)} %all_to_all.47.src), custom_call_target="tpu_custom_call" | custom-call | tf_op jit(solution)/shard_map/pallas_call | solution.py:62
  (8 shorter events, 0.2 us)
Async XLA Ops:
  3.1 61.4 %copy-start.1 = (f32[2,512,8]{1,2,0:T(8,128)S(1)}, f32[2,512,8]{1,2,0:T(8,128)}, u32[]{:S(2)}) copy-start(f32[2,512,8]{1,2,0:T(8,128)} %param.4) | copy-start | bytes 98308
  146.3 1.4 copy-start

commit v3 on v2

v3 whole, which is shorter than its diff:
```python
import jax
import jax.numpy as jnp
import numpy as np
from jax import lax
from jax.experimental import pallas as pl
from jax.experimental.pallas import tpu as pltpu
from jax.sharding import PartitionSpec as P

ITERS = 2
LANES = 128
INNER, ROWS, OUTER = ((1,), (0,)), ((1,), (1,)), ((0,), (0,))
VMEM = pl.BlockSpec(memory_space=pltpu.VMEM)
HBM = pl.BlockSpec(memory_space=pltpu.HBM)
DMA = pltpu.SemaphoreType.DMA


def params(mib):
    return pltpu.CompilerParams(vmem_limit_bytes=mib * 1024 * 1024)


def swap(value, axis):
    return lax.all_to_all(value, axis, split_axis=0, concat_axis=0, tiled=True)


def to_all(value, axis):
    count = lax.axis_size(axis)
    return swap(jnp.broadcast_to(value[None], (count,) + value.shape), axis)


def shape(*dims):
    return jax.ShapeDtypeStruct(dims, jnp.float32)


def dot(a, b, dims):
    return lax.dot_general(a, b, (dims, ((), ())), preferred_element_type=jnp.float32)


def cube_of(x_ref, s):
    parts, _, chans, pixels = x_ref.shape
    return x_ref[:, s].reshape(parts * chans, pixels)


def parts_of(value, count):
    parts = []
    for _ in range(count):
        part = value.astype(jnp.bfloat16)
        parts.append(part)
        value = value - part.astype(jnp.float32)
    return parts


def split_kernel(src, dst):
    step = dst.shape[3]
    for j in range(dst.shape[0]):
        dst[j] = src[:, :, j * step : (j + 1) * step]


def products(rows, x_parts, dims):
    count = rows.shape[0]
    stacked = [part.astype(jnp.float32) for part in parts_of(rows, 3)]
    stacked = jnp.concatenate(stacked, axis=0).astype(jnp.bfloat16)
    a = dot(stacked, x_parts[0], dims)
    b = dot(stacked[: 2 * count], x_parts[1], dims)
    c = dot(stacked[:count], x_parts[2], dims)
    return a[:count] + ((a[count : 2 * count] + b[:count]) + ((a[2 * count :] + b[count:]) + c))


def expand(rows, weights):
    left = [part.astype(jnp.float32) for part in parts_of(rows, 3)]
    right = [part.astype(jnp.float32) for part in parts_of(weights, 3)]
    pairs = [(0, 0), (0, 1), (1, 0), (0, 2), (1, 1), (2, 0)]
    left = jnp.concatenate([left[a] for a, _ in pairs], axis=0).astype(jnp.bfloat16)
    right = jnp.concatenate([right[b] for _, b in pairs], axis=0).astype(jnp.bfloat16)
    return dot(left, right, OUTER)


def grow(rows, x, scale, out_ref, s):
    modes = rows.shape[0]
    x_parts = parts_of(x, 3)
    weights = products(rows, x_parts, INNER) * scale
    grown = products(weights, x_parts, ROWS)
    for c in range(grown.shape[1] // LANES):
        out_ref[s * modes : (s + 1) * modes, c, :] = grown[:, c * LANES : (c + 1) * LANES]


def grown_rows(g_ref, s, modes):
    return jnp.concatenate([g_ref[s * modes : (s + 1) * modes, c, :] for c in range(g_ref.shape[1])], axis=1)


def orthonormal(rows):
    modes = rows.shape[0]
    index = lax.broadcasted_iota(jnp.int32, (modes, 1), 0)
    for j in range(modes - 1):
        pivot = rows[j : j + 1]
        prods = jnp.sum(rows * pivot, axis=1, keepdims=True)
        ratio = jnp.where(index > j, prods / prods[j : j + 1], 0.0)
        rows = rows - ratio * pivot
    norms = jnp.sum(rows * rows, axis=1, keepdims=True)
    inverse = lax.rsqrt(norms)
    inverse = inverse * (1.5 - 0.5 * norms * inverse * inverse)
    return rows * inverse


def first_kernel(scale, x_ref, start_ref, out_ref):
    for s in range(x_ref.shape[1]):
        grow(start_ref[s], cube_of(x_ref, s), scale, out_ref, s)


def next_kernel(scale, modes, x_ref, g_ref, out_ref):
    for s in range(x_ref.shape[1]):
        rows = orthonormal(grown_rows(g_ref, s, modes))
        grow(rows, cube_of(x_ref, s), scale, out_ref, s)


def last_kernel(modes, x_ref, g_ref, table_ref, out_ref, held, sem):
    copy = pltpu.make_async_copy(table_ref, held, sem)
    copy.start()
    owners, halves, _, waves, step = out_ref.shape
    count = held.shape[0] // 2
    bases = [orthonormal(grown_rows(g_ref, s, modes)) for s in range(x_ref.shape[1])]
    for s, rows in enumerate(bases):
        x = cube_of(x_ref, s)
        weights = products(rows, parts_of(x, 3), INNER)
        high, low = parts_of(x - expand(rows, weights), 2)
        if s == 0:
            copy.wait()
        a = dot(held[...], high, INNER)
        total = a[:count] + (a[count:] + dot(held[:count], low, INNER))
        out_ref[:, :, s] = total.reshape(owners, halves, waves, step)


def join_kernel(src, dst, held, sems):
    parts, halves, species, _, step = src.shape
    copies = []
    for h in range(halves):
        for s in range(species):
            for j in range(parts):
                held[h, s, :, j * step : (j + 1) * step] = src[j, h, s]
            copy = pltpu.make_async_copy(held.at[h, s], dst.at[h, s], sems.at[h, s])
            copy.start()
            copies.append(copy)
    for copy in copies:
        copy.wait()


def tables(owners, waves, width):
    k = np.arange(waves)[:, None]
    f = np.arange(width)[None, :]
    phase = 2.0 * np.pi * (k * f % width) / width
    both = np.stack([np.cos(phase), -np.sin(phase)]) / np.sqrt(width)
    rows = both.reshape(2, owners, waves // owners, width).transpose(1, 0, 2, 3).reshape(2 * waves, width)
    high = rows.astype(jnp.bfloat16)
    low = (rows - high.astype(np.float64)).astype(jnp.bfloat16)
    return np.concatenate([high, low])


def body(cubes, start_block):
    owners = lax.axis_size("chan")
    species, chans, pixels = cubes.shape
    width = chans * owners
    modes = start_block.shape[2]
    waves = width // 2
    step = pixels // owners
    scale = 1.0 / (pixels * lax.axis_size("pix"))
    share = shape(species * modes, width // LANES, LANES)

    def summed(part):
        row = jnp.sum(swap(part, "chan"), axis=0)
        row = jnp.sum(to_all(row, "pix"), axis=0)
        return to_all(row, "chan")

    split = pl.pallas_call(
        split_kernel,
        out_shape=shape(owners, species, chans, step), in_specs=[VMEM], out_specs=VMEM, compiler_params=params(4),
    )(cubes)
    x = swap(split, "chan")
    grown = pl.pallas_call(
        lambda *refs: first_kernel(scale, *refs),
        out_shape=share, in_specs=[VMEM, VMEM], out_specs=VMEM, compiler_params=params(24),
    )(x, jnp.swapaxes(start_block, 1, 2))
    grown = summed(grown)
    for _ in range(ITERS - 1):
        grown = pl.pallas_call(
            lambda *refs: next_kernel(scale, modes, *refs),
            out_shape=share, in_specs=[VMEM, VMEM], out_specs=VMEM, compiler_params=params(24),
        )(x, grown)
        grown = summed(grown)
    blocks = pl.pallas_call(
        lambda *refs: last_kernel(modes, *refs),
        out_shape=shape(owners, 2, species, waves // owners, step),
        in_specs=[VMEM, VMEM, HBM], out_specs=VMEM, compiler_params=params(24),
        scratch_shapes=[pltpu.VMEM((4 * waves, width), jnp.bfloat16), DMA],
    )(x, grown, jnp.asarray(tables(owners, waves, width)))
    return pl.pallas_call(
        join_kernel,
        out_shape=shape(2, species, waves // owners, pixels), in_specs=[VMEM], out_specs=HBM, compiler_params=params(8),
        scratch_shapes=[pltpu.VMEM((2, species, waves // owners, pixels), jnp.float32), DMA((2, species))],
    )(swap(blocks, "chan"))


def solution(mesh):
    placed = (P(None, "chan", "pix"), P())
    return jax.shard_map(
        body, mesh=mesh, in_specs=placed, out_specs=P(None, None, "chan", "pix"), check_vma=False
    )
```

time: 211 us -> 202 us (0.957)
  Pallas kernels: 17.9 us -> 9.08 us
    pallas_call x3, Pallas kernels: 11.5 us -> 5.31 us  [the longest x1 3.8 us: body(): pl.pallas_call(lambda *refs: last_kernel(modes, *refs), out_shape=shape(o...]
where the time goes in v3:
time: 202 us; the launch traced here: 201 us
  blocking collectives  190 us (94%)
  Pallas kernels  9.08 us (4%)
    all_to_all x8, blocking collectives, swap(): return lax.all_to_all(value, axis, split_axis=0, concat_axis=0, tiled=True)  190 us

profile of v3, /device:TPU:1, one launch (start us, length us, event | category | flops | bytes accessed | tf_op | source)
XLA Modules:
  0.0 201.2 jit_solution(1647401572313423230)
XLA Ops:
  0.0 0.0 copy-start
  0.0 1.6 copy-done
  1.6 0.1 shard_map.37
  1.7 0.0 copy-start.2
  1.7 60.4 %all_to_all.40.refs_0_ = f32[16,2,32,512]{3,2,1,0:T(8,128)S(1)} all-to-all(f32[16,2,32,512]{3,2,1,0:T(8,128)S(1)} %shard_map.37), channel_id=1, replica_groups=mesh['chan'=16,'pix'=32] {'chan'}, dimensions={0} | all-to-all | bytes 4194304 | tf_op jit(solution)/shard_map/all_to_all | solution.py:22
  62.1 0.0 copy-done.2
  62.1 0.0 copy-start.1
  62.1 1.5 shard_map.38
  63.7 10.1 %all_to_all.41 = f32[16,4,128]{2,1,0:T(4,128)S(1)} all-to-all(f32[16,4,128]{2,1,0:T(4,128)S(1)} %shard_map.38), channel_id=1, replica_groups=mesh['chan'=16,'pix'=32] {'chan'}, dimensions={0} | all-to-all | bytes 65536 | tf_op jit(solution)/shard_map/all_to_all | solution.py:22
  73.8 20.6 %all_to_all.42 = f32[32,4,128]{2,1,0:T(4,128)S(1)} all-to-all(f32[32,4,128]{2,1,0:T(4,128)S(1)} %broadcast_in_dim.8), channel_id=1, replica_groups=mesh['chan'=16,'pix'=32] {'pix'}, dimensions={0} | all-to-all | bytes 131072 | tf_op jit(solution)/shard_map/all_to_all | solution.py:22
  94.5 11.7 %all_to_all.43.refs_1_ = f32[16,4,128]{2,1,0:T(4,128)S(1)} all-to-all(f32[16,4,128]{2,1,0:T(4,128)S(1)} %broadcast_in_dim.9), channel_id=1, replica_groups=mesh['chan'=16,'pix'=32] {'chan'}, dimensions={0} | all-to-all | bytes 65536 | tf_op jit(solution)/shard_map/all_to_all | solution.py:22
  106.2 2.2 %shard_map.39 = f32[16,4,128]{2,1,0:T(4,128)S(1)} custom-call(f32[16,2,32,512]{3,2,1,0:T(8,128)S(1)} %all_to_all.40.refs_0_, f32[16,4,128]{2,1,0:T(4,128)S(1)} %all_to_all.43.refs_1_), custom_call_target="tpu_custom_call" | custom-call | tf_op jit(solution)/shard_map/pallas_call | solution.py:183
  108.4 10.3 %all_to_all.44 = f32[16,4,128]{2,1,0:T(4,128)S(1)} all-to-all(f32[16,4,128]{2,1,0:T(4,128)S(1)} %shard_map.39), channel_id=1, replica_groups=mesh['chan'=16,'pix'=32] {'chan'}, dimensions={0} | all-to-all | bytes 65536 | tf_op jit(solution)/shard_map/all_to_all | solution.py:22
  118.7 11.9 %all_to_all.45 = f32[32,4,128]{2,1,0:T(4,128)S(1)} all-to-all(f32[32,4,128]{2,1,0:T(4,128)S(1)} %broadcast_in_dim.10), channel_id=1, replica_groups=mesh['chan'=16,'pix'=32] {'pix'}, dimensions={0} | all-to-all | bytes 131072 | tf_op jit(solution)/shard_map/all_to_all | solution.py:22
  130.6 11.5 %all_to_all.46.refs_1_ = f32[16,4,128]{2,1,0:T(4,128)S(1)} all-to-all(f32[16,4,128]{2,1,0:T(4,128)S(1)} %broadcast_in_dim.11), channel_id=1, replica_groups=mesh['chan'=16,'pix'=32] {'chan'}, dimensions={0} | all-to-all | bytes 65536 | tf_op jit(solution)/shard_map/all_to_all | solution.py:22
  142.2 0.0 copy-done.1
  142.2 3.8 %shard_map.40 = f32[16,2,2,16,512]{4,3,2,1,0:T(8,128)S(1)} custom-call(f32[16,2,32,512]{3,2,1,0:T(8,128)S(1)} %all_to_all.40.refs_0_, f32[16,4,128]{2,1,0:T(4,128)S(1)} %all_to_all.46.refs_1_, bf16[1024,512]{1,0:T(8,128)(2,1)S(1)} %copy-done.1), custom_call_target="tpu_custom_call" | custom-call | tf_op jit(solution)/shard_map/pallas_call | solution.py:188
  146.0 53.9 %all_to_all.47.src = f32[16,2,2,16,512]{4,3,2,1,0:T(8,128)S(1)} all-to-all(f32[16,2,2,16,512]{4,3,2,1,0:T(8,128)S(1)} %shard_map.40), channel_id=1, replica_groups=mesh['chan'=16,'pix'=32] {'chan'}, dimensions={0} | all-to-all | bytes 4194304 | tf_op jit(solution)/shard_map/all_to_all | solution.py:22
  199.9 1.4 shard_map.41
  (8 shorter events, 0.2 us)
Async XLA Ops:
  0.0 1.6 copy-start
  1.7 60.4 %copy-start.2 = (f32[2,512,8]{1,2,0:T(8,128)S(1)}, f32[2,512,8]{1,2,0:T(8,128)}, u32[]{:S(2)}) copy-start(f32[2,512,8]{1,2,0:T(8,128)} %param.4) | copy-start | bytes 98308
  62.1 80.0 %copy-start.1 = (bf16[1024,512]{1,0:T(8,128)(2,1)S(1)}, bf16[1024,512]{1,0:T(8,128)(2,1)}, u32[]{:S(2)}) copy-start(bf16[1024,512]{1,0:T(8,128)(2,1)} %constant.4.clone.refs_2_) | copy-start | bytes 3145732

commit v4 on v3

v4 whole, which is shorter than its diff:
```python
import jax
import jax.numpy as jnp
import numpy as np
from jax import lax
from jax.experimental import pallas as pl
from jax.experimental.pallas import tpu as pltpu
from jax.sharding import PartitionSpec as P

ITERS = 2
LANES = 128
GROUPS = 4
INNER, ROWS, OUTER = ((1,), (0,)), ((1,), (1,)), ((0,), (0,))
VMEM = pl.BlockSpec(memory_space=pltpu.VMEM)
HBM = pl.BlockSpec(memory_space=pltpu.HBM)
DMA = pltpu.SemaphoreType.DMA


def params(mib):
    return pltpu.CompilerParams(vmem_limit_bytes=mib * 1024 * 1024)


def swap(value, axis):
    return lax.all_to_all(value, axis, split_axis=0, concat_axis=0, tiled=True)


def to_all(value, axis):
    count = lax.axis_size(axis)
    return swap(jnp.broadcast_to(value[None], (count,) + value.shape), axis)


def after(value, others):
    return lax.optimization_barrier((value, others))


def cost(flops, moved):
    return pl.CostEstimate(flops=flops, bytes_accessed=moved, transcendentals=0)


def shape(*dims):
    return jax.ShapeDtypeStruct(dims, jnp.float32)


def dot(a, b, dims):
    return lax.dot_general(a, b, (dims, ((), ())), preferred_element_type=jnp.float32)


def cube_of(x_ref, s):
    parts, _, chans, pixels = x_ref.shape
    return x_ref[:, s].reshape(parts * chans, pixels)


def turned_cube(x_ref, s):
    owners, _, rows, pixels = x_ref.shape
    step = rows // GROUPS
    groups = [x_ref[:, s, q * step : (q + 1) * step].reshape(owners * step, pixels) for q in range(GROUPS)]
    return jnp.concatenate(groups, axis=0)


def store_turned(out_ref, value, s):
    owners, _, rows, pixels = out_ref.shape
    step = rows // GROUPS
    for q in range(GROUPS):
        part = value[q * owners * step : (q + 1) * owners * step]
        out_ref[:, s, q * step : (q + 1) * step] = part.reshape(owners, step, pixels)


def folded(value, axis):
    half = value.shape[axis] // 2
    first, second = lax.slice_in_dim(value, 0, half, axis=axis), lax.slice_in_dim(value, half, 2 * half, axis=axis)
    return first + second, first - second


def parts_of(value, count):
    parts = []
    for _ in range(count):
        part = value.astype(jnp.bfloat16)
        parts.append(part)
        value = value - part.astype(jnp.float32)
    return parts


def split_kernel(src, dst):
    step = dst.shape[3]
    for j in range(dst.shape[0]):
        dst[j] = src[:, :, j * step : (j + 1) * step]


def products_of_parts(left, right, dims):
    count = left[0].shape[0]
    stacked = jnp.concatenate(left, axis=0)
    a = dot(stacked, right[0], dims)
    b = dot(stacked[: 2 * count], right[1], dims)
    c = dot(stacked[:count], right[2], dims)
    return a[:count] + ((a[count : 2 * count] + b[:count]) + ((a[2 * count :] + b[count:]) + c))


def products(rows, right, dims):
    count = rows.shape[0]
    stacked = jnp.concatenate([part.astype(jnp.float32) for part in parts_of(rows, 3)], axis=0).astype(jnp.bfloat16)
    a = dot(stacked, right[0], dims)
    b = dot(stacked[: 2 * count], right[1], dims)
    c = dot(stacked[:count], right[2], dims)
    return a[:count] + ((a[count : 2 * count] + b[:count]) + ((a[2 * count :] + b[count:]) + c))


def expand(rows, weights):
    left = [part.astype(jnp.float32) for part in parts_of(rows, 3)]
    right = [part.astype(jnp.float32) for part in parts_of(weights, 3)]
    pairs = [(0, 0), (0, 1), (1, 0), (0, 2), (1, 1), (2, 0)]
    left = jnp.concatenate([left[a] for a, _ in pairs], axis=0).astype(jnp.bfloat16)
    right = jnp.concatenate([right[b] for _, b in pairs], axis=0).astype(jnp.bfloat16)
    return dot(left, right, OUTER)


def store_rows(out_ref, rows, s):
    modes = rows.shape[0]
    for c in range(rows.shape[1] // LANES):
        out_ref[s * modes : (s + 1) * modes, c, :] = rows[:, c * LANES : (c + 1) * LANES]


def grown_rows(g_ref, s, modes):
    return jnp.concatenate([g_ref[s * modes : (s + 1) * modes, c, :] for c in range(g_ref.shape[1])], axis=1)


def inverse_factor(rows):
    modes = rows.shape[0]
    index = lax.broadcasted_iota(jnp.int32, (modes, 1), 0)
    taken = lax.broadcasted_iota(jnp.int32, (modes, LANES), 0) == lax.broadcasted_iota(jnp.int32, (modes, LANES), 1)
    taken = taken.astype(jnp.float32)
    for j in range(modes - 1):
        pivot = rows[j : j + 1]
        prods = jnp.sum(rows * pivot, axis=1, keepdims=True)
        ratio = jnp.where(index > j, prods / prods[j : j + 1], 0.0)
        rows = rows - ratio * pivot
        taken = taken - ratio * taken[j : j + 1]
    norms = jnp.sum(rows * rows, axis=1, keepdims=True)
    inverse = lax.rsqrt(norms)
    inverse = inverse * (1.5 - 0.5 * norms * inverse * inverse)
    return taken * inverse


def mixed(factor, rows):
    total = factor[:, 0:1] * rows[0:1]
    for j in range(1, rows.shape[0]):
        total = total + factor[:, j : j + 1] * rows[j : j + 1]
    return total


def first_kernel(scale, x_ref, start_ref, table_ref, out_ref):
    grown = []
    for s in range(x_ref.shape[1]):
        x_parts = parts_of(cube_of(x_ref, s), 3)
        weights = products(start_ref[s], x_parts, INNER) * scale
        grown.append(products(weights, x_parts, ROWS))
    turned = [
        products(rows, [table_ref[p, parity] for p in range(3)], ROWS)
        for parity, rows in enumerate(folded(jnp.concatenate(grown, axis=0), 1))
    ]
    half = turned[0].shape[1] // 2
    turned = [turned[q % 2][:, q // 2 * half : (q // 2 + 1) * half] for q in range(GROUPS)]
    store_rows(out_ref, jnp.concatenate(turned, axis=1), 0)


def transform_kernel(x_ref, table_ref, out_ref):
    for s in range(x_ref.shape[1]):
        halves = []
        for parity, x in enumerate(folded(cube_of(x_ref, s), 0)):
            halves.append(products_of_parts([table_ref[p, parity] for p in range(3)], parts_of(x, 3), INNER))
        half = halves[0].shape[0] // 2
        turned = [halves[q % 2][q // 2 * half : (q // 2 + 1) * half] for q in range(GROUPS)]
        store_turned(out_ref, jnp.concatenate(turned, axis=0), s)


def next_kernel(scale, modes, x_ref, g_ref, out_ref):
    species = range(x_ref.shape[1])
    grown = [grown_rows(g_ref, s, modes) for s in species]
    x_parts = [parts_of(turned_cube(x_ref, s), 3) for s in species]
    raised = [products(rows, parts, INNER) for rows, parts in zip(grown, x_parts)]
    factors = [inverse_factor(rows) for rows in grown]
    for s in species:
        store_rows(out_ref, products(mixed(factors[s], raised[s]) * scale, x_parts[s], ROWS), s)


def last_kernel(modes, x_ref, g_ref, out_ref):
    owners, _, tiles, rows, _ = out_ref.shape
    count = rows // GROUPS
    species = range(x_ref.shape[1])
    grown = [grown_rows(g_ref, s, modes) for s in species]
    cubes = [turned_cube(x_ref, s) for s in species]
    raised = [products(rows, parts_of(x, 3), INNER) for x, rows in zip(cubes, grown)]
    factors = [inverse_factor(rows) for rows in grown]
    for s in species:
        fix = expand(mixed(factors[s], grown[s]), mixed(factors[s], raised[s]))
        cleaned = cubes[s] - fix
        scaled = cleaned * np.float32(np.sqrt(0.5))
        for q in range(GROUPS):
            rows = pl.ds(q // 2 * count * 2 + q % 2, count, stride=2)
            for c in range(tiles):
                part = scaled[q * owners * count : (q + 1) * owners * count, c * LANES : (c + 1) * LANES]
                out_ref[:, s, c, rows, :] = part.reshape(owners, count, LANES)
        for c in range(tiles):
            out_ref[0, s, c, 0:1, :] = cleaned[0:1, c * LANES : (c + 1) * LANES]
            out_ref[0, s, c, 2 * count : 2 * count + 1, :] = jnp.zeros((1, LANES), jnp.float32)


def join_kernel(src, dst, held, sems):
    halves, species, waves, _ = dst.shape
    copies = []
    for h in range(halves):
        for s in range(species):
            for j in range(src.shape[0]):
                for c in range(src.shape[2]):
                    at = (j * src.shape[2] + c) * LANES
                    held[h, s, :, at : at + LANES] = src[j, s, c, h * waves : (h + 1) * waves]
            copy = pltpu.make_async_copy(held.at[h, s], dst.at[h, s], sems.at[h, s])
            copy.start()
            copies.append(copy)
    for copy in copies:
        copy.wait()


def tables(owners, waves, width):
    k = np.arange(waves)[:, None]
    f = np.arange(width // 2)[None, :]
    phase = 2.0 * np.pi * (k * f % width) / width
    both = np.stack([np.cos(phase), -np.sin(phase)]) * np.sqrt(2.0 / width)
    both[0, 0] = 1.0 / np.sqrt(width)
    both[1, 0] = (1.0 - 2.0 * (f[0] % 2)) / np.sqrt(width)
    left = both.reshape(2, owners, waves // owners // 2, 2, width // 2).transpose(3, 0, 1, 2, 4).reshape(2, waves, width // 2)
    parts = []
    for _ in range(3):
        part = left.astype(jnp.bfloat16)
        parts.append(part)
        left = left - part.astype(np.float64)
    return np.stack(parts)


def body(cubes, start_block):
    owners = lax.axis_size("chan")
    species, chans, pixels = cubes.shape
    width = chans * owners
    modes = start_block.shape[2]
    waves = width // 2
    step = pixels // owners
    scale = 1.0 / (pixels * lax.axis_size("pix"))
    share = shape(species * modes, width // LANES, LANES)
    split_shape = shape(owners, species, chans, step)
    table = jnp.asarray(tables(owners, waves, width))
    work = 2 * species * width * step
    grant = params(24)

    split = pl.pallas_call(
        split_kernel,
        out_shape=split_shape, in_specs=[VMEM], out_specs=VMEM, compiler_params=params(4),
    )(cubes)
    x = swap(split, "chan")
    part = pl.pallas_call(
        lambda *refs: first_kernel(scale, *refs),
        out_shape=share, in_specs=[VMEM, VMEM, VMEM], out_specs=VMEM, compiler_params=grant,
        cost_estimate=cost(12 * modes * work, work),
    )(x, jnp.swapaxes(start_block, 1, 2), table)

    row = jnp.sum(swap(part, "chan"), axis=0)
    row, given = after(row, x)
    x = pl.pallas_call(
        transform_kernel,
        out_shape=split_shape, in_specs=[VMEM, VMEM], out_specs=VMEM, input_output_aliases={0: 0},
        compiler_params=grant, cost_estimate=cost(6 * waves * work, 6 * work),
    )(given, table)
    row = jnp.sum(to_all(row, "pix"), axis=0)
    row, x = after(row, x)
    grown = to_all(row, "chan")
    for _ in range(ITERS - 1):
        part = pl.pallas_call(
            lambda *refs: next_kernel(scale, modes, *refs),
            out_shape=share, in_specs=[VMEM, VMEM], out_specs=VMEM, compiler_params=grant,
        )(x, grown)
        row = jnp.sum(swap(part, "chan"), axis=0)
        row = jnp.sum(to_all(row, "pix"), axis=0)
        grown = to_all(row, "chan")
    blocks = pl.pallas_call(
        lambda *refs: last_kernel(modes, *refs),
        out_shape=shape(owners, species, step // LANES, chans, LANES), in_specs=[VMEM, VMEM], out_specs=VMEM, compiler_params=grant,
    )(x, grown)
    return pl.pallas_call(
        join_kernel,
        out_shape=shape(2, species, waves // owners, pixels), in_specs=[VMEM], out_specs=HBM, compiler_params=params(8),
        scratch_shapes=[pltpu.VMEM((2, species, waves // owners, pixels), jnp.float32), DMA((2, species))],
    )(swap(blocks, "chan"))


def solution(mesh):
    placed = (P(None, "chan", "pix"), P())
    return jax.shard_map(
        body, mesh=mesh, in_specs=placed, out_specs=P(None, None, "chan", "pix"), check_vma=False
    )
```

time: 202 us -> 201 us (level)
  blocking collectives: 190 us -> 170 us
  starting transfers between devices: 0 us -> 11.9 us
  waiting for transfers between devices: 0 us -> 7.02 us
    all_to_all x8 -> x7, blocking collectives: 190 us -> 170 us  [swap(): return lax.all_to_all(value, axis, split_axis=0, concat_axis=0, tiled=True)]
    all_to_all x0 -> x1, starting transfers between devices: none -> 11.9 us  [swap(): return lax.all_to_all(value, axis, split_axis=0, concat_axis=0, tiled=True)]
    all_to_all x0 -> x1, waiting for transfers between devices: none -> 7.02 us  [swap(): return lax.all_to_all(value, axis, split_axis=0, concat_axis=0, tiled=True)]
    pallas_call x1, Pallas kernels: 3.8 us -> 1.55 us  [body(): pl.pallas_call(lambda *refs: last_kernel(modes, *refs), out_shape=shape(o...]
  transfers between devices with their start and end apart: 0 -> 1, of which waited for: 0 -> 1; matrix products, arithmetic and copies ran while one was open for 0% -> 0% of each run, Pallas kernels for 0% -> 1%
where the time goes in v4:
time: 201 us; the launch traced here: 200 us
  blocking collectives  170 us (85%)
  starting transfers between devices  11.9 us (6%)
  Pallas kernels  8.76 us (4%)
  waiting for transfers between devices  7.02 us (3%)
  local copies, waits for them, and re-layouts  2.28 us (1%)
    all_to_all x7, blocking collectives, swap(): return lax.all_to_all(value, axis, split_axis=0, concat_axis=0, tiled=True)  170 us
    all_to_all x1, starting transfers between devices, swap(): return lax.all_to_all(value, axis, split_axis=0, concat_axis=0, tiled=True)  11.9 us
    all_to_all x1, waiting for transfers between devices, swap(): return lax.all_to_all(value, axis, split_axis=0, concat_axis=0, tiled=True)  7.02 us
  transfers between devices with their start and end apart: 1, of which 1 were waited for; matrix products, arithmetic and copies ran while one was open for 0% of the time, Pallas kernels for 1%

profile of v4, /device:TPU:1, one launch (start us, length us, event | category | flops | bytes accessed | tf_op | source)
XLA Modules:
  0.0 200.1 jit_solution(13475190826824346370)
XLA Ops:
  0.0 0.0 copy-start
  0.0 1.6 copy-done
  1.6 0.1 shard_map.37
  1.7 0.0 copy-start.1
  1.7 0.0 copy-start.2
  1.8 60.5 %all_to_all.40.refs_0_.x_ref = f32[16,2,32,512]{3,2,1,0:T(8,128)S(1)} all-to-all(f32[16,2,32,512]{3,2,1,0:T(8,128)S(1)} %shard_map.37), channel_id=1, replica_groups=mesh['chan'=16,'pix'=32] {'chan'}, dimensions={0} | all-to-all | bytes 4194304 | tf_op jit(solution)/shard_map/all_to_all | solution.py:23
  62.3 0.0 copy-done.1
  62.3 0.0 copy-done.2
  62.3 1.8 shard_map.38
  64.1 10.1 %all_to_all.41 = f32[16,4,128]{2,1,0:T(4,128)S(1)} all-to-all(f32[16,4,128]{2,1,0:T(4,128)S(1)} %shard_map.38), channel_id=1, replica_groups=mesh['chan'=16,'pix'=32] {'chan'}, dimensions={0} | all-to-all | bytes 65536 | tf_op jit(solution)/shard_map/all_to_all | solution.py:23
  74.2 0.6 broadcast_in_dim.8
  74.9 11.9 %all-to-all-start.2 = ((f32[32,4,128]{2,1,0:T(4,128)}), f32[32,4,128]{2,1,0:T(4,128)S(1)}, u32[]{:S(2)}, u32[]{:S(2)}) async-start(f32[32,4,128]{2,1,0:T(4,128)} %broadcast_in_dim.8), calls=%async_computation.2 | async-start | bytes 131072 | tf_op jit(solution)/shard_map/all_to_all | solution.py:23
  86.8 1.8 shard_map.39.refs_0_
  88.6 7.0 %all-to-all-done.2 = f32[32,4,128]{2,1,0:T(4,128)S(1)} async-done(((f32[32,4,128]{2,1,0:T(4,128)}), f32[32,4,128]{2,1,0:T(4,128)S(1)}, u32[]{:S(2)}, u32[]{:S(2)}) %all-to-all-start.2) | async-done | bytes 65568 | tf_op jit(solution)/shard_map/all_to_all | solution.py:23
  95.7 11.7 %all_to_all.42.refs_1_ = f32[16,4,128]{2,1,0:T(4,128)S(1)} all-to-all(f32[16,4,128]{2,1,0:T(4,128)S(1)} %broadcast_in_dim.9), channel_id=1, replica_groups=mesh['chan'=16,'pix'=32] {'chan'}, dimensions={0} | all-to-all | bytes 65536 | tf_op jit(solution)/shard_map/all_to_all | solution.py:23
  107.4 2.0 %shard_map.40 = f32[16,4,128]{2,1,0:T(4,128)S(1)} custom-call(f32[16,2,32,512]{3,2,1,0:T(8,128)S(1)} %shard_map.39.refs_0_, f32[16,4,128]{2,1,0:T(4,128)S(1)} %all_to_all.42.refs_1_), custom_call_target="tpu_custom_call" | custom-call | tf_op jit(solution)/shard_map/pallas_call | solution.py:274
  109.5 10.3 %all_to_all.43 = f32[16,4,128]{2,1,0:T(4,128)S(1)} all-to-all(f32[16,4,128]{2,1,0:T(4,128)S(1)} %shard_map.40), channel_id=1, replica_groups=mesh['chan'=16,'pix'=32] {'chan'}, dimensions={0} | all-to-all | bytes 65536 | tf_op jit(solution)/shard_map/all_to_all | solution.py:23
  119.8 11.9 %all_to_all.44 = f32[32,4,128]{2,1,0:T(4,128)S(1)} all-to-all(f32[32,4,128]{2,1,0:T(4,128)S(1)} %broadcast_in_dim.10), channel_id=1, replica_groups=mesh['chan'=16,'pix'=32] {'pix'}, dimensions={0} | all-to-all | bytes 131072 | tf_op jit(solution)/shard_map/all_to_all | solution.py:23
  131.7 11.5 %all_to_all.45.refs_1_ = f32[16,4,128]{2,1,0:T(4,128)S(1)} all-to-all(f32[16,4,128]{2,1,0:T(4,128)S(1)} %broadcast_in_dim.11), channel_id=1, replica_groups=mesh['chan'=16,'pix'=32] {'chan'}, dimensions={0} | all-to-all | bytes 65536 | tf_op jit(solution)/shard_map/all_to_all | solution.py:23
  143.2 1.5 shard_map.41
  144.8 53.9 %all_to_all.46.src = f32[16,2,4,32,128]{4,3,2,1,0:T(8,128)S(1)} all-to-all(f32[16,2,4,32,128]{4,3,2,1,0:T(8,128)S(1)} %shard_map.41), channel_id=1, replica_groups=mesh['chan'=16,'pix'=32] {'chan'}, dimensions={0} | all-to-all | bytes 4194304 | tf_op jit(solution)/shard_map/all_to_all | solution.py:23
  198.7 1.4 shard_map.42
  (7 shorter events, 0.2 us)
Async XLA Ops:
  0.0 1.6 copy-start
  1.7 60.5 %copy-start.1 = (bf16[3,2,256,256]{3,2,1,0:T(8,128)(2,1)S(1)}, bf16[3,2,256,256]{3,2,1,0:T(8,128)(2,1)}, u32[]{:S(2)}) copy-start(bf16[3,2,256,256]{3,2,1,0:T(8,128)(2,1)} %constant.4.clone.refs_2_.table_ref) | copy-start | bytes 2359300
  1.7 60.5 %copy-start.2 = (f32[2,512,8]{1,2,0:T(8,128)S(1)}, f32[2,512,8]{1,2,0:T(8,128)}, u32[]{:S(2)}) copy-start(f32[2,512,8]{1,2,0:T(8,128)} %param.4) | copy-start | bytes 98308
  74.9 20.8 %all-to-all-start.2 = ((f32[32,4,128]{2,1,0:T(4,128)}), f32[32,4,128]{2,1,0:T(4,128)S(1)}, u32[]{:S(2)}, u32[]{:S(2)}) async-start(f32[32,4,128]{2,1,0:T(4,128)} %broadcast_in_dim.8), calls=%async_computation.2 | async-start | bytes 131072 | tf_op jit(solution)/shard_map/all_to_all | solution.py:23

commit v5 on v4

--- a/solution.py
+++ b/solution.py
@@ -6,7 +6,6 @@
 from jax.experimental.pallas import tpu as pltpu
 from jax.sharding import PartitionSpec as P
 
-ITERS = 2
 LANES = 128
 GROUPS = 4
 INNER, ROWS, OUTER = ((1,), (0,)), ((1,), (1,)), ((0,), (0,))
@@ -146,19 +145,19 @@
     return total
 
 
-def first_kernel(scale, x_ref, start_ref, table_ref, out_ref):
-    grown = []
+def first_kernel(scale, x_ref, start_ref, out_ref):
     for s in range(x_ref.shape[1]):
         x_parts = parts_of(cube_of(x_ref, s), 3)
         weights = products(start_ref[s], x_parts, INNER) * scale
-        grown.append(products(weights, x_parts, ROWS))
+        store_rows(out_ref, products(weights, x_parts, ROWS), s)
+
+
+def turned_rows(rows, table_ref):
     turned = [
-        products(rows, [table_ref[p, parity] for p in range(3)], ROWS)
-        for parity, rows in enumerate(folded(jnp.concatenate(grown, axis=0), 1))
+        products(half, [table_ref[p, parity] for p in range(3)], ROWS) for parity, half in enumerate(folded(rows, 1))
     ]
     half = turned[0].shape[1] // 2
-    turned = [turned[q % 2][:, q // 2 * half : (q // 2 + 1) * half] for q in range(GROUPS)]
-    store_rows(out_ref, jnp.concatenate(turned, axis=1), 0)
+    return jnp.concatenate([turned[q % 2][:, q // 2 * half : (q // 2 + 1) * half] for q in range(GROUPS)], axis=1)
 
 
 def transform_kernel(x_ref, table_ref, out_ref):
@@ -171,17 +170,18 @@
         store_turned(out_ref, jnp.concatenate(turned, axis=0), s)
 
 
-def next_kernel(scale, modes, x_ref, g_ref, out_ref):
+def second_kernel(scale, modes, x_ref, g_ref, table_ref, out_ref):
     species = range(x_ref.shape[1])
     grown = [grown_rows(g_ref, s, modes) for s in species]
     x_parts = [parts_of(turned_cube(x_ref, s), 3) for s in species]
-    raised = [products(rows, parts, INNER) for rows, parts in zip(grown, x_parts)]
+    turned = turned_rows(jnp.concatenate(grown, axis=0), table_ref)
+    raised = [products(turned[s * modes : (s + 1) * modes], x_parts[s], INNER) for s in species]
     factors = [inverse_factor(rows) for rows in grown]
     for s in species:
         store_rows(out_ref, products(mixed(factors[s], raised[s]) * scale, x_parts[s], ROWS), s)
 
 
-def last_kernel(modes, x_ref, g_ref, out_ref):
+def last_kernel(modes, x_ref, g_ref, out_ref, held):
     owners, _, tiles, rows, _ = out_ref.shape
     count = rows // GROUPS
     species = range(x_ref.shape[1])
@@ -197,7 +197,8 @@
             rows = pl.ds(q // 2 * count * 2 + q % 2, count, stride=2)
             for c in range(tiles):
                 part = scaled[q * owners * count : (q + 1) * owners * count, c * LANES : (c + 1) * LANES]
-                out_ref[:, s, c, rows, :] = part.reshape(owners, count, LANES)
+                held[s, :, c, rows, :] = part.reshape(owners, count, LANES)
+        out_ref[:, s] = held[s, :, :, : count * GROUPS]
         for c in range(tiles):
             out_ref[0, s, c, 0:1, :] = cleaned[0:1, c * LANES : (c + 1) * LANES]
             out_ref[0, s, c, 2 * count : 2 * count + 1, :] = jnp.zeros((1, LANES), jnp.float32)
@@ -256,9 +257,9 @@
     x = swap(split, "chan")
     part = pl.pallas_call(
         lambda *refs: first_kernel(scale, *refs),
-        out_shape=share, in_specs=[VMEM, VMEM, VMEM], out_specs=VMEM, compiler_params=grant,
+        out_shape=share, in_specs=[VMEM, VMEM], out_specs=VMEM, compiler_params=grant,
         cost_estimate=cost(12 * modes * work, work),
-    )(x, jnp.swapaxes(start_block, 1, 2), table)
+    )(x, jnp.swapaxes(start_block, 1, 2))
 
     row = jnp.sum(swap(part, "chan"), axis=0)
     row, given = after(row, x)
@@ -270,17 +271,17 @@
     row = jnp.sum(to_all(row, "pix"), axis=0)
     row, x = after(row, x)
     grown = to_all(row, "chan")
-    for _ in range(ITERS - 1):
-        part = pl.pallas_call(
-            lambda *refs: next_kernel(scale, modes, *refs),
-            out_shape=share, in_specs=[VMEM, VMEM], out_specs=VMEM, compiler_params=grant,
-        )(x, grown)
-        row = jnp.sum(swap(part, "chan"), axis=0)
-        row = jnp.sum(to_all(row, "pix"), axis=0)
-        grown = to_all(row, "chan")
+    part = pl.pallas_call(
+        lambda *refs: second_kernel(scale, modes, *refs),
+        out_shape=share, in_specs=[VMEM, VMEM, VMEM], out_specs=VMEM, compiler_params=grant,
+    )(x, grown, table)
+    row = jnp.sum(swap(part, "chan"), axis=0)
+    row = jnp.sum(to_all(row, "pix"), axis=0)
+    grown = to_all(row, "chan")
     blocks = pl.pallas_call(
         lambda *refs: last_kernel(modes, *refs),
         out_shape=shape(owners, species, step // LANES, chans, LANES), in_specs=[VMEM, VMEM], out_specs=VMEM, compiler_params=grant,
+        scratch_shapes=[pltpu.VMEM((species, owners, step // LANES, chans + 8, LANES), jnp.float32)],
     )(x, grown)
     return pl.pallas_call(
         join_kernel,

time: 201 us -> 200 us (level)
  no operation moved by 1% of the time
where the time goes in v5:
time: 200 us
  blocking collectives  170 us (85%)
  starting transfers between devices  11.9 us (6%)
  Pallas kernels  8.65 us (4%)
  waiting for transfers between devices  7.01 us (4%)
  local copies, waits for them, and re-layouts  2.27 us (1%)
    all_to_all x7, blocking collectives, swap(): return lax.all_to_all(value, axis, split_axis=0, concat_axis=0, tiled=True)  170 us
    all_to_all x1, starting transfers between devices, swap(): return lax.all_to_all(value, axis, split_axis=0, concat_axis=0, tiled=True)  11.9 us
    all_to_all x1, waiting for transfers between devices, swap(): return lax.all_to_all(value, axis, split_axis=0, concat_axis=0, tiled=True)  7.01 us
  transfers between devices with their start and end apart: 1, of which 1 were waited for; matrix products, arithmetic and copies ran while one was open for 0% of the time, Pallas kernels for 1%

profile of v5, /device:TPU:1, one launch (start us, length us, event | category | flops | bytes accessed | tf_op | source)
XLA Modules:
  0.0 199.8 jit_solution(12652139640914533645)
XLA Ops:
  0.0 0.0 copy-start
  0.0 1.6 copy-done
  1.6 0.1 shard_map.37
  1.7 0.0 copy-start.2
  1.7 60.4 %all_to_all.40.refs_0_.x_ref = f32[16,2,32,512]{3,2,1,0:T(8,128)S(1)} all-to-all(f32[16,2,32,512]{3,2,1,0:T(8,128)S(1)} %shard_map.37), channel_id=1, replica_groups=mesh['chan'=16,'pix'=32] {'chan'}, dimensions={0} | all-to-all | bytes 4194304 | tf_op jit(solution)/shard_map/all_to_all | solution.py:22
  62.1 0.0 copy-start.1
  62.1 0.0 copy-done.2
  62.1 1.5 shard_map.38
  63.7 10.1 %all_to_all.41 = f32[16,4,128]{2,1,0:T(4,128)S(1)} all-to-all(f32[16,4,128]{2,1,0:T(4,128)S(1)} %shard_map.38), channel_id=1, replica_groups=mesh['chan'=16,'pix'=32] {'chan'}, dimensions={0} | all-to-all | bytes 65536 | tf_op jit(solution)/shard_map/all_to_all | solution.py:22
  73.8 0.6 broadcast_in_dim.8
  74.5 11.9 %all-to-all-start.2 = ((f32[32,4,128]{2,1,0:T(4,128)}), f32[32,4,128]{2,1,0:T(4,128)S(1)}, u32[]{:S(2)}, u32[]{:S(2)}) async-start(f32[32,4,128]{2,1,0:T(4,128)} %broadcast_in_dim.8), calls=%async_computation.2 | async-start | bytes 131072 | tf_op jit(solution)/shard_map/all_to_all | solution.py:22
  86.4 0.0 copy-done.1
  86.4 1.8 shard_map.39.refs_0_
  88.2 7.0 %all-to-all-done.2 = f32[32,4,128]{2,1,0:T(4,128)S(1)} async-done(((f32[32,4,128]{2,1,0:T(4,128)}), f32[32,4,128]{2,1,0:T(4,128)S(1)}, u32[]{:S(2)}, u32[]{:S(2)}) %all-to-all-start.2) | async-done | bytes 65568 | tf_op jit(solution)/shard_map/all_to_all | solution.py:22
  95.3 11.7 %all_to_all.42.refs_1_ = f32[16,4,128]{2,1,0:T(4,128)S(1)} all-to-all(f32[16,4,128]{2,1,0:T(4,128)S(1)} %broadcast_in_dim.9), channel_id=1, replica_groups=mesh['chan'=16,'pix'=32] {'chan'}, dimensions={0} | all-to-all | bytes 65536 | tf_op jit(solution)/shard_map/all_to_all | solution.py:22
  107.0 2.1 %shard_map.40 = f32[16,4,128]{2,1,0:T(4,128)S(1)} custom-call(f32[16,2,32,512]{3,2,1,0:T(8,128)S(1)} %shard_map.39.refs_0_, f32[16,4,128]{2,1,0:T(4,128)S(1)} %all_to_all.42.refs_1_, bf16[3,2,256,256]{3,2,1,0:T(8,128)(2,1)S(1)} %copy-done.1), custom_call_target="tpu_custom_call" | custom-call | tf_op jit(solution)/shard_map/pallas_call | solution.py:274
  109.1 10.3 %all_to_all.43 = f32[16,4,128]{2,1,0:T(4,128)S(1)} all-to-all(f32[16,4,128]{2,1,0:T(4,128)S(1)} %shard_map.40), channel_id=1, replica_groups=mesh['chan'=16,'pix'=32] {'chan'}, dimensions={0} | all-to-all | bytes 65536 | tf_op jit(solution)/shard_map/all_to_all | solution.py:22
  119.4 11.9 %all_to_all.44 = f32[32,4,128]{2,1,0:T(4,128)S(1)} all-to-all(f32[32,4,128]{2,1,0:T(4,128)S(1)} %broadcast_in_dim.10), channel_id=1, replica_groups=mesh['chan'=16,'pix'=32] {'pix'}, dimensions={0} | all-to-all | bytes 131072 | tf_op jit(solution)/shard_map/all_to_all | solution.py:22
  131.4 11.5 %all_to_all.45.refs_1_ = f32[16,4,128]{2,1,0:T(4,128)S(1)} all-to-all(f32[16,4,128]{2,1,0:T(4,128)S(1)} %broadcast_in_dim.11), channel_id=1, replica_groups=mesh['chan'=16,'pix'=32] {'chan'}, dimensions={0} | all-to-all | bytes 65536 | tf_op jit(solution)/shard_map/all_to_all | solution.py:22
  142.9 1.6 shard_map.41
  144.5 53.9 %all_to_all.46.src = f32[16,2,4,32,128]{4,3,2,1,0:T(8,128)S(1)} all-to-all(f32[16,2,4,32,128]{4,3,2,1,0:T(8,128)S(1)} %shard_map.41), channel_id=1, replica_groups=mesh['chan'=16,'pix'=32] {'chan'}, dimensions={0} | all-to-all | bytes 4194304 | tf_op jit(solution)/shard_map/all_to_all | solution.py:22
  198.4 1.4 shard_map.42
  (7 shorter events, 0.2 us)
Async XLA Ops:
  0.0 1.6 copy-start
  1.7 60.4 %copy-start.2 = (f32[2,512,8]{1,2,0:T(8,128)S(1)}, f32[2,512,8]{1,2,0:T(8,128)}, u32[]{:S(2)}) copy-start(f32[2,512,8]{1,2,0:T(8,128)} %param.4) | copy-start | bytes 98308
  62.1 24.3 %copy-start.1 = (bf16[3,2,256,256]{3,2,1,0:T(8,128)(2,1)S(1)}, bf16[3,2,256,256]{3,2,1,0:T(8,128)(2,1)}, u32[]{:S(2)}) copy-start(bf16[3,2,256,256]{3,2,1,0:T(8,128)(2,1)} %constant.4.clone.table_ref.refs_2_) | copy-start | bytes 2359300
  74.5 20.8 %all-to-all-start.2 = ((f32[32,4,128]{2,1,0:T(4,128)}), f32[32,4,128]{2,1,0:T(4,128)S(1)}, u32[]{:S(2)}, u32[]{:S(2)}) async-start(f32[32,4,128]{2,1,0:T(4,128)} %broadcast_in_dim.8), calls=%async_computation.2 | async-start | bytes 131072 | tf_op jit(solution)/shard_map/all_to_all | solution.py:22

commit v6 on v4

--- a/solution.py
+++ b/solution.py
@@ -122,28 +122,18 @@
     return jnp.concatenate([g_ref[s * modes : (s + 1) * modes, c, :] for c in range(g_ref.shape[1])], axis=1)
 
 
-def inverse_factor(rows):
+def orthonormal(rows):
     modes = rows.shape[0]
     index = lax.broadcasted_iota(jnp.int32, (modes, 1), 0)
-    taken = lax.broadcasted_iota(jnp.int32, (modes, LANES), 0) == lax.broadcasted_iota(jnp.int32, (modes, LANES), 1)
-    taken = taken.astype(jnp.float32)
     for j in range(modes - 1):
         pivot = rows[j : j + 1]
         prods = jnp.sum(rows * pivot, axis=1, keepdims=True)
         ratio = jnp.where(index > j, prods / prods[j : j + 1], 0.0)
         rows = rows - ratio * pivot
-        taken = taken - ratio * taken[j : j + 1]
     norms = jnp.sum(rows * rows, axis=1, keepdims=True)
     inverse = lax.rsqrt(norms)
     inverse = inverse * (1.5 - 0.5 * norms * inverse * inverse)
-    return taken * inverse
-
-
-def mixed(factor, rows):
-    total = factor[:, 0:1] * rows[0:1]
-    for j in range(1, rows.shape[0]):
-        total = total + factor[:, j : j + 1] * rows[j : j + 1]
-    return total
+    return rows * inverse
 
 
 def first_kernel(scale, x_ref, start_ref, table_ref, out_ref):
@@ -173,31 +163,30 @@
 
 def next_kernel(scale, modes, x_ref, g_ref, out_ref):
     species = range(x_ref.shape[1])
-    grown = [grown_rows(g_ref, s, modes) for s in species]
+    bases = [orthonormal(grown_rows(g_ref, s, modes)) for s in species]
     x_parts = [parts_of(turned_cube(x_ref, s), 3) for s in species]
-    raised = [products(rows, parts, INNER) for rows, parts in zip(grown, x_parts)]
-    factors = [inverse_factor(rows) for rows in grown]
+    weights = [products(basis, parts, INNER) * scale for basis, parts in zip(bases, x_parts)]
     for s in species:
-        store_rows(out_ref, products(mixed(factors[s], raised[s]) * scale, x_parts[s], ROWS), s)
-
-
-def last_kernel(modes, x_ref, g_ref, out_ref):
+        store_rows(out_ref, products(weights[s], x_parts[s], ROWS), s)
+
+
+def last_kernel(modes, x_ref, g_ref, out_ref, held):
     owners, _, tiles, rows, _ = out_ref.shape
     count = rows // GROUPS
     species = range(x_ref.shape[1])
-    grown = [grown_rows(g_ref, s, modes) for s in species]
+    bases = [orthonormal(grown_rows(g_ref, s, modes)) for s in species]
     cubes = [turned_cube(x_ref, s) for s in species]
-    raised = [products(rows, parts_of(x, 3), INNER) for x, rows in zip(cubes, grown)]
-    factors = [inverse_factor(rows) for rows in grown]
+    weights = [products(basis, parts_of(x, 3), INNER) for basis, x in zip(bases, cubes)]
     for s in species:
-        fix = expand(mixed(factors[s], grown[s]), mixed(factors[s], raised[s]))
+        fix = expand(bases[s], weights[s])
         cleaned = cubes[s] - fix
         scaled = cleaned * np.float32(np.sqrt(0.5))
         for q in range(GROUPS):
             rows = pl.ds(q // 2 * count * 2 + q % 2, count, stride=2)
             for c in range(tiles):
                 part = scaled[q * owners * count : (q + 1) * owners * count, c * LANES : (c + 1) * LANES]
-                out_ref[:, s, c, rows, :] = part.reshape(owners, count, LANES)
+                held[s, :, c, rows, :] = part.reshape(owners, count, LANES)
+        out_ref[:, s] = held[s, :, :, : count * GROUPS]
         for c in range(tiles):
             out_ref[0, s, c, 0:1, :] = cleaned[0:1, c * LANES : (c + 1) * LANES]
             out_ref[0, s, c, 2 * count : 2 * count + 1, :] = jnp.zeros((1, LANES), jnp.float32)
@@ -281,6 +270,7 @@
     blocks = pl.pallas_call(
         lambda *refs: last_kernel(modes, *refs),
         out_shape=shape(owners, species, step // LANES, chans, LANES), in_specs=[VMEM, VMEM], out_specs=VMEM, compiler_params=grant,
+        scratch_shapes=[pltpu.VMEM((species, owners, step // LANES, chans + 8, LANES), jnp.float32)],
     )(x, grown)
     return pl.pallas_call(
         join_kernel,

time: 201 us -> 201 us (level)
  no operation moved by 1% of the time
where the time goes in v6:
time: 201 us; the launch traced here: 200 us
  blocking collectives  170 us (85%)
  starting transfers between devices  11.9 us (6%)
  Pallas kernels  9.15 us (5%)
  waiting for transfers between devices  7.02 us (3%)
  local copies, waits for them, and re-layouts  2.28 us (1%)
    all_to_all x7, blocking collectives, swap(): return lax.all_to_all(value, axis, split_axis=0, concat_axis=0, tiled=True)  170 us
    all_to_all x1, starting transfers between devices, swap(): return lax.all_to_all(value, axis, split_axis=0, concat_axis=0, tiled=True)  11.9 us
    all_to_all x1, waiting for transfers between devices, swap(): return lax.all_to_all(value, axis, split_axis=0, concat_axis=0, tiled=True)  7.02 us
  transfers between devices with their start and end apart: 1, of which 1 were waited for; matrix products, arithmetic and copies ran while one was open for 0% of the time, Pallas kernels for 1%

profile of v6, /device:TPU:1, one launch (start us, length us, event | category | flops | bytes accessed | tf_op | source)
XLA Modules:
  0.0 200.5 jit_solution(9175658720156455930)
XLA Ops:
  0.0 0.0 copy-start
  0.0 1.6 copy-done
  1.6 0.1 shard_map.37
  1.7 0.0 copy-start.1
  1.7 0.0 copy-start.2
  1.8 60.5 %all_to_all.40.refs_0_.x_ref = f32[16,2,32,512]{3,2,1,0:T(8,128)S(1)} all-to-all(f32[16,2,32,512]{3,2,1,0:T(8,128)S(1)} %shard_map.37), channel_id=1, replica_groups=mesh['chan'=16,'pix'=32] {'chan'}, dimensions={0} | all-to-all | bytes 4194304 | tf_op jit(solution)/shard_map/all_to_all | solution.py:23
  62.3 0.0 copy-done.1
  62.3 0.0 copy-done.2
  62.3 1.8 shard_map.38
  64.1 10.1 %all_to_all.41 = f32[16,4,128]{2,1,0:T(4,128)S(1)} all-to-all(f32[16,4,128]{2,1,0:T(4,128)S(1)} %shard_map.38), channel_id=1, replica_groups=mesh['chan'=16,'pix'=32] {'chan'}, dimensions={0} | all-to-all | bytes 65536 | tf_op jit(solution)/shard_map/all_to_all | solution.py:23
  74.2 0.6 broadcast_in_dim.8
  74.9 11.9 %all-to-all-start.2 = ((f32[32,4,128]{2,1,0:T(4,128)}), f32[32,4,128]{2,1,0:T(4,128)S(1)}, u32[]{:S(2)}, u32[]{:S(2)}) async-start(f32[32,4,128]{2,1,0:T(4,128)} %broadcast_in_dim.8), calls=%async_computation.2 | async-start | bytes 131072 | tf_op jit(solution)/shard_map/all_to_all | solution.py:23
  86.8 1.8 shard_map.39.refs_0_
  88.6 7.0 %all-to-all-done.2 = f32[32,4,128]{2,1,0:T(4,128)S(1)} async-done(((f32[32,4,128]{2,1,0:T(4,128)}), f32[32,4,128]{2,1,0:T(4,128)S(1)}, u32[]{:S(2)}, u32[]{:S(2)}) %all-to-all-start.2) | async-done | bytes 65568 | tf_op jit(solution)/shard_map/all_to_all | solution.py:23
  95.7 11.7 %all_to_all.42.refs_1_ = f32[16,4,128]{2,1,0:T(4,128)S(1)} all-to-all(f32[16,4,128]{2,1,0:T(4,128)S(1)} %broadcast_in_dim.9), channel_id=1, replica_groups=mesh['chan'=16,'pix'=32] {'chan'}, dimensions={0} | all-to-all | bytes 65536 | tf_op jit(solution)/shard_map/all_to_all | solution.py:23
  107.4 2.2 %shard_map.40 = f32[16,4,128]{2,1,0:T(4,128)S(1)} custom-call(f32[16,2,32,512]{3,2,1,0:T(8,128)S(1)} %shard_map.39.refs_0_, f32[16,4,128]{2,1,0:T(4,128)S(1)} %all_to_all.42.refs_1_), custom_call_target="tpu_custom_call" | custom-call | tf_op jit(solution)/shard_map/pallas_call | solution.py:263
  109.6 10.3 %all_to_all.43 = f32[16,4,128]{2,1,0:T(4,128)S(1)} all-to-all(f32[16,4,128]{2,1,0:T(4,128)S(1)} %shard_map.40), channel_id=1, replica_groups=mesh['chan'=16,'pix'=32] {'chan'}, dimensions={0} | all-to-all | bytes 65536 | tf_op jit(solution)/shard_map/all_to_all | solution.py:23
  119.9 11.9 %all_to_all.44 = f32[32,4,128]{2,1,0:T(4,128)S(1)} all-to-all(f32[32,4,128]{2,1,0:T(4,128)S(1)} %broadcast_in_dim.10), channel_id=1, replica_groups=mesh['chan'=16,'pix'=32] {'pix'}, dimensions={0} | all-to-all | bytes 131072 | tf_op jit(solution)/shard_map/all_to_all | solution.py:23
  131.9 11.5 %all_to_all.45.refs_1_ = f32[16,4,128]{2,1,0:T(4,128)S(1)} all-to-all(f32[16,4,128]{2,1,0:T(4,128)S(1)} %broadcast_in_dim.11), channel_id=1, replica_groups=mesh['chan'=16,'pix'=32] {'chan'}, dimensions={0} | all-to-all | bytes 65536 | tf_op jit(solution)/shard_map/all_to_all | solution.py:23
  143.4 1.8 shard_map.41
  145.2 53.9 %all_to_all.46.src = f32[16,2,4,32,128]{4,3,2,1,0:T(8,128)S(1)} all-to-all(f32[16,2,4,32,128]{4,3,2,1,0:T(8,128)S(1)} %shard_map.41), channel_id=1, replica_groups=mesh['chan'=16,'pix'=32] {'chan'}, dimensions={0} | all-to-all | bytes 4194304 | tf_op jit(solution)/shard_map/all_to_all | solution.py:23
  199.1 1.4 shard_map.42
  (7 shorter events, 0.2 us)
Async XLA Ops:
  0.0 1.6 copy-start
  1.7 60.5 %copy-start.1 = (bf16[3,2,256,256]{3,2,1,0:T(8,128)(2,1)S(1)}, bf16[3,2,256,256]{3,2,1,0:T(8,128)(2,1)}, u32[]{:S(2)}) copy-start(bf16[3,2,256,256]{3,2,1,0:T(8,128)(2,1)} %constant.4.clone.refs_2_.table_ref) | copy-start | bytes 2359300
  1.7 60.5 %copy-start.2 = (f32[2,512,8]{1,2,0:T(8,128)S(1)}, f32[2,512,8]{1,2,0:T(8,128)}, u32[]{:S(2)}) copy-start(f32[2,512,8]{1,2,0:T(8,128)} %param.4) | copy-start | bytes 98308
  74.9 20.8 %all-to-all-start.2 = ((f32[32,4,128]{2,1,0:T(4,128)}), f32[32,4,128]{2,1,0:T(4,128)S(1)}, u32[]{:S(2)}, u32[]{:S(2)}) async-start(f32[32,4,128]{2,1,0:T(4,128)} %broadcast_in_dim.8), calls=%async_computation.2 | async-start | bytes 131072 | tf_op jit(solution)/shard_map/all_to_all | solution.py:23

commit v7 on v5

--- a/solution.py
+++ b/solution.py
@@ -119,6 +119,20 @@
 
 def grown_rows(g_ref, s, modes):
     return jnp.concatenate([g_ref[s * modes : (s + 1) * modes, c, :] for c in range(g_ref.shape[1])], axis=1)
+
+
+def orthonormal(rows):
+    modes = rows.shape[0]
+    index = lax.broadcasted_iota(jnp.int32, (modes, 1), 0)
+    for j in range(modes - 1):
+        pivot = rows[j : j + 1]
+        prods = jnp.sum(rows * pivot, axis=1, keepdims=True)
+        ratio = jnp.where(index > j, prods / prods[j : j + 1], 0.0)
+        rows = rows - ratio * pivot
+    norms = jnp.sum(rows * rows, axis=1, keepdims=True)
+    inverse = lax.rsqrt(norms)
+    inverse = inverse * (1.5 - 0.5 * norms * inverse * inverse)
+    return rows * inverse
 
 
 def inverse_factor(rows):
@@ -173,24 +187,23 @@
 def second_kernel(scale, modes, x_ref, g_ref, table_ref, out_ref):
     species = range(x_ref.shape[1])
     grown = [grown_rows(g_ref, s, modes) for s in species]
+    turned = turned_rows(jnp.concatenate(grown, axis=0), table_ref)
     x_parts = [parts_of(turned_cube(x_ref, s), 3) for s in species]
-    turned = turned_rows(jnp.concatenate(grown, axis=0), table_ref)
-    raised = [products(turned[s * modes : (s + 1) * modes], x_parts[s], INNER) for s in species]
-    factors = [inverse_factor(rows) for rows in grown]
+    bases = [mixed(inverse_factor(grown[s]), turned[s * modes : (s + 1) * modes]) for s in species]
+    weights = [products(basis, parts, INNER) * scale for basis, parts in zip(bases, x_parts)]
     for s in species:
-        store_rows(out_ref, products(mixed(factors[s], raised[s]) * scale, x_parts[s], ROWS), s)
+        store_rows(out_ref, products(weights[s], x_parts[s], ROWS), s)
 
 
 def last_kernel(modes, x_ref, g_ref, out_ref, held):
     owners, _, tiles, rows, _ = out_ref.shape
     count = rows // GROUPS
     species = range(x_ref.shape[1])
-    grown = [grown_rows(g_ref, s, modes) for s in species]
+    bases = [orthonormal(grown_rows(g_ref, s, modes)) for s in species]
     cubes = [turned_cube(x_ref, s) for s in species]
-    raised = [products(rows, parts_of(x, 3), INNER) for x, rows in zip(cubes, grown)]
-    factors = [inverse_factor(rows) for rows in grown]
+    weights = [products(basis, parts_of(x, 3), INNER) for basis, x in zip(bases, cubes)]
     for s in species:
-        fix = expand(mixed(factors[s], grown[s]), mixed(factors[s], raised[s]))
+        fix = expand(bases[s], weights[s])
         cleaned = cubes[s] - fix
         scaled = cleaned * np.float32(np.sqrt(0.5))
         for q in range(GROUPS):

time: 200 us -> 201 us (level)
  no operation moved by 1% of the time
where the time goes in v7:
time: 201 us; the launch traced here: 200 us
  blocking collectives  170 us (85%)
  starting transfers between devices  11.9 us (6%)
  Pallas kernels  9.03 us (4%)
  waiting for transfers between devices  7.01 us (3%)
  local copies, waits for them, and re-layouts  2.27 us (1%)
    all_to_all x7, blocking collectives, swap(): return lax.all_to_all(value, axis, split_axis=0, concat_axis=0, tiled=True)  170 us
    all_to_all x1, starting transfers between devices, swap(): return lax.all_to_all(value, axis, split_axis=0, concat_axis=0, tiled=True)  11.9 us
    all_to_all x1, waiting for transfers between devices, swap(): return lax.all_to_all(value, axis, split_axis=0, concat_axis=0, tiled=True)  7.01 us
  transfers between devices with their start and end apart: 1, of which 1 were waited for; matrix products, arithmetic and copies ran while one was open for 0% of the time, Pallas kernels for 1%

profile of v7, /device:TPU:1, one launch (start us, length us, event | category | flops | bytes accessed | tf_op | source)
XLA Modules:
  0.0 200.2 jit_solution(5929075417497070698)
XLA Ops:
  0.0 0.0 copy-start
  0.0 1.6 copy-done
  1.6 0.1 shard_map.37
  1.7 0.0 copy-start.2
  1.7 60.4 %all_to_all.40.refs_0_.x_ref = f32[16,2,32,512]{3,2,1,0:T(8,128)S(1)} all-to-all(f32[16,2,32,512]{3,2,1,0:T(8,128)S(1)} %shard_map.37), channel_id=1, replica_groups=mesh['chan'=16,'pix'=32] {'chan'}, dimensions={0} | all-to-all | bytes 4194304 | tf_op jit(solution)/shard_map/all_to_all | solution.py:22
  62.1 0.0 copy-start.1
  62.1 0.0 copy-done.2
  62.1 1.5 shard_map.38
  63.7 10.1 %all_to_all.41 = f32[16,4,128]{2,1,0:T(4,128)S(1)} all-to-all(f32[16,4,128]{2,1,0:T(4,128)S(1)} %shard_map.38), channel_id=1, replica_groups=mesh['chan'=16,'pix'=32] {'chan'}, dimensions={0} | all-to-all | bytes 65536 | tf_op jit(solution)/shard_map/all_to_all | solution.py:22
  73.8 0.6 broadcast_in_dim.8
  74.5 11.9 %all-to-all-start.2 = ((f32[32,4,128]{2,1,0:T(4,128)}), f32[32,4,128]{2,1,0:T(4,128)S(1)}, u32[]{:S(2)}, u32[]{:S(2)}) async-start(f32[32,4,128]{2,1,0:T(4,128)} %broadcast_in_dim.8), calls=%async_computation.2 | async-start | bytes 131072 | tf_op jit(solution)/shard_map/all_to_all | solution.py:22
  86.4 0.0 copy-done.1
  86.4 1.8 shard_map.39.refs_0_
  88.2 7.0 %all-to-all-done.2 = f32[32,4,128]{2,1,0:T(4,128)S(1)} async-done(((f32[32,4,128]{2,1,0:T(4,128)}), f32[32,4,128]{2,1,0:T(4,128)S(1)}, u32[]{:S(2)}, u32[]{:S(2)}) %all-to-all-start.2) | async-done | bytes 65568 | tf_op jit(solution)/shard_map/all_to_all | solution.py:22
  95.3 11.7 %all_to_all.42.refs_1_ = f32[16,4,128]{2,1,0:T(4,128)S(1)} all-to-all(f32[16,4,128]{2,1,0:T(4,128)S(1)} %broadcast_in_dim.9), channel_id=1, replica_groups=mesh['chan'=16,'pix'=32] {'chan'}, dimensions={0} | all-to-all | bytes 65536 | tf_op jit(solution)/shard_map/all_to_all | solution.py:22
  107.0 2.4 %shard_map.40 = f32[16,4,128]{2,1,0:T(4,128)S(1)} custom-call(f32[16,2,32,512]{3,2,1,0:T(8,128)S(1)} %shard_map.39.refs_0_, f32[16,4,128]{2,1,0:T(4,128)S(1)} %all_to_all.42.refs_1_, bf16[3,2,256,256]{3,2,1,0:T(8,128)(2,1)S(1)} %copy-done.1), custom_call_target="tpu_custom_call" | custom-call | tf_op jit(solution)/shard_map/pallas_call | solution.py:287
  109.4 10.3 %all_to_all.43 = f32[16,4,128]{2,1,0:T(4,128)S(1)} all-to-all(f32[16,4,128]{2,1,0:T(4,128)S(1)} %shard_map.40), channel_id=1, replica_groups=mesh['chan'=16,'pix'=32] {'chan'}, dimensions={0} | all-to-all | bytes 65536 | tf_op jit(solution)/shard_map/all_to_all | solution.py:22
  119.7 11.9 %all_to_all.44 = f32[32,4,128]{2,1,0:T(4,128)S(1)} all-to-all(f32[32,4,128]{2,1,0:T(4,128)S(1)} %broadcast_in_dim.10), channel_id=1, replica_groups=mesh['chan'=16,'pix'=32] {'pix'}, dimensions={0} | all-to-all | bytes 131072 | tf_op jit(solution)/shard_map/all_to_all | solution.py:22
  131.6 11.5 %all_to_all.45.refs_1_ = f32[16,4,128]{2,1,0:T(4,128)S(1)} all-to-all(f32[16,4,128]{2,1,0:T(4,128)S(1)} %broadcast_in_dim.11), channel_id=1, replica_groups=mesh['chan'=16,'pix'=32] {'chan'}, dimensions={0} | all-to-all | bytes 65536 | tf_op jit(solution)/shard_map/all_to_all | solution.py:22
  143.1 1.8 shard_map.41
  144.9 53.9 %all_to_all.46.src = f32[16,2,4,32,128]{4,3,2,1,0:T(8,128)S(1)} all-to-all(f32[16,2,4,32,128]{4,3,2,1,0:T(8,128)S(1)} %shard_map.41), channel_id=1, replica_groups=mesh['chan'=16,'pix'=32] {'chan'}, dimensions={0} | all-to-all | bytes 4194304 | tf_op jit(solution)/shard_map/all_to_all | solution.py:22
  198.8 1.4 shard_map.42
  (7 shorter events, 0.2 us)
Async XLA Ops:
  0.0 1.6 copy-start
  1.7 60.4 %copy-start.2 = (f32[2,512,8]{1,2,0:T(8,128)S(1)}, f32[2,512,8]{1,2,0:T(8,128)}, u32[]{:S(2)}) copy-start(f32[2,512,8]{1,2,0:T(8,128)} %param.4) | copy-start | bytes 98308
  62.1 24.3 %copy-start.1 = (bf16[3,2,256,256]{3,2,1,0:T(8,128)(2,1)S(1)}, bf16[3,2,256,256]{3,2,1,0:T(8,128)(2,1)}, u32[]{:S(2)}) copy-start(bf16[3,2,256,256]{3,2,1,0:T(8,128)(2,1)} %constant.4.clone.table_ref.refs_2_) | copy-start | bytes 2359300
  74.5 20.8 %all-to-all-start.2 = ((f32[32,4,128]{2,1,0:T(4,128)}), f32[32,4,128]{2,1,0:T(4,128)S(1)}, u32[]{:S(2)}, u32[]{:S(2)}) async-start(f32[32,4,128]{2,1,0:T(4,128)} %broadcast_in_dim.8), calls=%async_computation.2 | async-start | bytes 131072 | tf_op jit(solution)/shard_map/all_to_all | solution.py:22

commit v8 on v7

--- a/solution.py
+++ b/solution.py
@@ -274,15 +274,15 @@
         cost_estimate=cost(12 * modes * work, work),
     )(x, jnp.swapaxes(start_block, 1, 2))
 
+    part, given = after(part, x)
     row = jnp.sum(swap(part, "chan"), axis=0)
-    row, given = after(row, x)
     x = pl.pallas_call(
         transform_kernel,
         out_shape=split_shape, in_specs=[VMEM, VMEM], out_specs=VMEM, input_output_aliases={0: 0},
         compiler_params=grant, cost_estimate=cost(6 * waves * work, 6 * work),
     )(given, table)
+    row, x = after(row, x)
     row = jnp.sum(to_all(row, "pix"), axis=0)
-    row, x = after(row, x)
     grown = to_all(row, "chan")
     part = pl.pallas_call(
         lambda *refs: second_kernel(scale, modes, *refs),

time: 201 us -> 201 us (level)
  blocking collectives: 170 us -> 180 us
  starting transfers between devices: 11.9 us -> 3.39 us
    all_to_all x7, blocking collectives: 170 us -> 180 us  [swap(): return lax.all_to_all(value, axis, split_axis=0, concat_axis=0, tiled=True)]
    all_to_all x1, starting transfers between devices: 11.9 us -> 3.39 us  [swap(): return lax.all_to_all(value, axis, split_axis=0, concat_axis=0, tiled=True)]
where the time goes in v8:
time: 201 us; the launch traced here: 200 us
  blocking collectives  180 us (90%)
  Pallas kernels  9.66 us (5%)
  waiting for transfers between devices  5.06 us (3%)
  starting transfers between devices  3.39 us (2%)
    all_to_all x7, blocking collectives, swap(): return lax.all_to_all(value, axis, split_axis=0, concat_axis=0, tiled=True)  180 us
    all_to_all x1, waiting for transfers between devices, swap(): return lax.all_to_all(value, axis, split_axis=0, concat_axis=0, tiled=True)  5.06 us
  transfers between devices with their start and end apart: 1, of which 1 were waited for; matrix products, arithmetic and copies ran while one was open for 0% of the time, Pallas kernels for 1%

profile of v8, /device:TPU:1, one launch (start us, length us, event | category | flops | bytes accessed | tf_op | source)
XLA Modules:
  0.0 200.2 jit_solution(6204307961793706800)
XLA Ops:
  0.0 0.0 copy-start
  0.0 1.6 copy-done
  1.6 0.1 shard_map.37
  1.7 0.0 copy-start.2
  1.7 60.4 %all_to_all.40.refs_0_.x_ref = f32[16,2,32,512]{3,2,1,0:T(8,128)S(1)} all-to-all(f32[16,2,32,512]{3,2,1,0:T(8,128)S(1)} %shard_map.37), channel_id=1, replica_groups=mesh['chan'=16,'pix'=32] {'chan'}, dimensions={0} | all-to-all | bytes 4194304 | tf_op jit(solution)/shard_map/all_to_all | solution.py:22
  62.1 0.0 copy-start.1
  62.1 0.0 copy-done.2
  62.1 2.2 %shard_map.38 = f32[16,4,128]{2,1,0:T(4,128)} custom-call(f32[16,2,32,512]{3,2,1,0:T(8,128)S(1)} %all_to_all.40.refs_0_.x_ref, f32[2,8,512]{2,1,0:T(8,128)S(1)} %bitcast.1), custom_call_target="tpu_custom_call" | custom-call | flops 100663296 | bytes 1048576 | tf_op jit(solution)/shard_map/pallas_call | solution.py:271
  64.3 3.4 %all-to-all-start.1 = ((f32[16,4,128]{2,1,0:T(4,128)}), f32[16,4,128]{2,1,0:T(4,128)S(1)}, u32[]{:S(2)}, u32[]{:S(2)}) async-start(f32[16,4,128]{2,1,0:T(4,128)} %shard_map.38), calls=%async_computation.1 | async-start | bytes 65536 | tf_op jit(solution)/shard_map/all_to_all | solution.py:22
  67.7 0.0 copy-done.1
  67.7 1.8 shard_map.39.refs_0_
  69.5 5.1 %all-to-all-done.1 = f32[16,4,128]{2,1,0:T(4,128)S(1)} async-done(((f32[16,4,128]{2,1,0:T(4,128)}), f32[16,4,128]{2,1,0:T(4,128)S(1)}, u32[]{:S(2)}, u32[]{:S(2)}) %all-to-all-start.1) | async-done | bytes 32800 | tf_op jit(solution)/shard_map/all_to_all | solution.py:22
  74.7 20.6 %all_to_all.41 = f32[32,4,128]{2,1,0:T(4,128)S(1)} all-to-all(f32[32,4,128]{2,1,0:T(4,128)S(1)} %broadcast_in_dim.8), channel_id=1, replica_groups=mesh['chan'=16,'pix'=32] {'pix'}, dimensions={0} | all-to-all | bytes 131072 | tf_op jit(solution)/shard_map/all_to_all | solution.py:22
  95.3 11.7 %all_to_all.42.refs_1_ = f32[16,4,128]{2,1,0:T(4,128)S(1)} all-to-all(f32[16,4,128]{2,1,0:T(4,128)S(1)} %broadcast_in_dim.9), channel_id=1, replica_groups=mesh['chan'=16,'pix'=32] {'chan'}, dimensions={0} | all-to-all | bytes 65536 | tf_op jit(solution)/shard_map/all_to_all | solution.py:22
  107.0 2.4 %shard_map.40 = f32[16,4,128]{2,1,0:T(4,128)S(1)} custom-call(f32[16,2,32,512]{3,2,1,0:T(8,128)S(1)} %shard_map.39.refs_0_, f32[16,4,128]{2,1,0:T(4,128)S(1)} %all_to_all.42.refs_1_, bf16[3,2,256,256]{3,2,1,0:T(8,128)(2,1)S(1)} %copy-done.1), custom_call_target="tpu_custom_call" | custom-call | tf_op jit(solution)/shard_map/pallas_call | solution.py:287
  109.4 10.3 %all_to_all.43 = f32[16,4,128]{2,1,0:T(4,128)S(1)} all-to-all(f32[16,4,128]{2,1,0:T(4,128)S(1)} %shard_map.40), channel_id=1, replica_groups=mesh['chan'=16,'pix'=32] {'chan'}, dimensions={0} | all-to-all | bytes 65536 | tf_op jit(solution)/shard_map/all_to_all | solution.py:22
  119.7 11.9 %all_to_all.44 = f32[32,4,128]{2,1,0:T(4,128)S(1)} all-to-all(f32[32,4,128]{2,1,0:T(4,128)S(1)} %broadcast_in_dim.10), channel_id=1, replica_groups=mesh['chan'=16,'pix'=32] {'pix'}, dimensions={0} | all-to-all | bytes 131072 | tf_op jit(solution)/shard_map/all_to_all | solution.py:22
  131.6 11.5 %all_to_all.45.refs_1_ = f32[16,4,128]{2,1,0:T(4,128)S(1)} all-to-all(f32[16,4,128]{2,1,0:T(4,128)S(1)} %broadcast_in_dim.11), channel_id=1, replica_groups=mesh['chan'=16,'pix'=32] {'chan'}, dimensions={0} | all-to-all | bytes 65536 | tf_op jit(solution)/shard_map/all_to_all | solution.py:22
  143.1 1.8 shard_map.41
  144.9 53.9 %all_to_all.46.src = f32[16,2,4,32,128]{4,3,2,1,0:T(8,128)S(1)} all-to-all(f32[16,2,4,32,128]{4,3,2,1,0:T(8,128)S(1)} %shard_map.41), channel_id=1, replica_groups=mesh['chan'=16,'pix'=32] {'chan'}, dimensions={0} | all-to-all | bytes 4194304 | tf_op jit(solution)/shard_map/all_to_all | solution.py:22
  198.8 1.4 shard_map.42
  (8 shorter events, 0.2 us)
Async XLA Ops:
  0.0 1.6 copy-start
  1.7 60.4 %copy-start.2 = (f32[2,512,8]{1,2,0:T(8,128)S(1)}, f32[2,512,8]{1,2,0:T(8,128)}, u32[]{:S(2)}) copy-start(f32[2,512,8]{1,2,0:T(8,128)} %param.4) | copy-start | bytes 98308
  62.1 5.6 %copy-start.1 = (bf16[3,2,256,256]{3,2,1,0:T(8,128)(2,1)S(1)}, bf16[3,2,256,256]{3,2,1,0:T(8,128)(2,1)}, u32[]{:S(2)}) copy-start(bf16[3,2,256,256]{3,2,1,0:T(8,128)(2,1)} %constant.4.clone.table_ref.refs_2_) | copy-start | bytes 2359300
  64.3 10.3 %all-to-all-start.1 = ((f32[16,4,128]{2,1,0:T(4,128)}), f32[16,4,128]{2,1,0:T(4,128)S(1)}, u32[]{:S(2)}, u32[]{:S(2)}) async-start(f32[16,4,128]{2,1,0:T(4,128)} %shard_map.38), calls=%async_computation.1 | async-start | bytes 65536 | tf_op jit(solution)/shard_map/all_to_all | solution.py:22

commit v9 on v8

--- a/solution.py
+++ b/solution.py
@@ -195,7 +195,7 @@
         store_rows(out_ref, products(weights[s], x_parts[s], ROWS), s)
 
 
-def last_kernel(modes, x_ref, g_ref, out_ref, held):
+def last_kernel(modes, x_ref, g_ref, out_ref):
     owners, _, tiles, rows, _ = out_ref.shape
     count = rows // GROUPS
     species = range(x_ref.shape[1])
@@ -210,8 +210,7 @@
             rows = pl.ds(q // 2 * count * 2 + q % 2, count, stride=2)
             for c in range(tiles):
                 part = scaled[q * owners * count : (q + 1) * owners * count, c * LANES : (c + 1) * LANES]
-                held[s, :, c, rows, :] = part.reshape(owners, count, LANES)
-        out_ref[:, s] = held[s, :, :, : count * GROUPS]
+                out_ref[:, s, c, rows, :] = part.reshape(owners, count, LANES)
         for c in range(tiles):
             out_ref[0, s, c, 0:1, :] = cleaned[0:1, c * LANES : (c + 1) * LANES]
             out_ref[0, s, c, 2 * count : 2 * count + 1, :] = jnp.zeros((1, LANES), jnp.float32)
@@ -294,7 +293,6 @@
     blocks = pl.pallas_call(
         lambda *refs: last_kernel(modes, *refs),
         out_shape=shape(owners, species, step // LANES, chans, LANES), in_specs=[VMEM, VMEM], out_specs=VMEM, compiler_params=grant,
-        scratch_shapes=[pltpu.VMEM((species, owners, step // LANES, chans + 8, LANES), jnp.float32)],
     )(x, grown)
     return pl.pallas_call(
         join_kernel,

time: 201 us -> 201 us (level)
  no operation moved by 1% of the time
where the time goes in v9:
time: 201 us; the launch traced here: 200 us
  blocking collectives  180 us (90%)
  Pallas kernels  9.61 us (5%)
  waiting for transfers between devices  5.06 us (3%)
  starting transfers between devices  3.39 us (2%)
    all_to_all x7, blocking collectives, swap(): return lax.all_to_all(value, axis, split_axis=0, concat_axis=0, tiled=True)  180 us
    all_to_all x1, waiting for transfers between devices, swap(): return lax.all_to_all(value, axis, split_axis=0, concat_axis=0, tiled=True)  5.06 us
  transfers between devices with their start and end apart: 1, of which 1 were waited for; matrix products, arithmetic and copies ran while one was open for 0% of the time, Pallas kernels for 1%

profile of v9, /device:TPU:1, one launch (start us, length us, event | category | flops | bytes accessed | tf_op | source)
XLA Modules:
  0.0 200.1 jit_solution(17849772266733278581)
XLA Ops:
  0.0 0.0 copy-start
  0.0 1.6 copy-done
  1.6 0.1 shard_map.37
  1.7 0.0 copy-start.2
  1.7 60.4 %all_to_all.40.refs_0_.x_ref = f32[16,2,32,512]{3,2,1,0:T(8,128)S(1)} all-to-all(f32[16,2,32,512]{3,2,1,0:T(8,128)S(1)} %shard_map.37), channel_id=1, replica_groups=mesh['chan'=16,'pix'=32] {'chan'}, dimensions={0} | all-to-all | bytes 4194304 | tf_op jit(solution)/shard_map/all_to_all | solution.py:22
  62.1 0.0 copy-start.1
  62.1 0.0 copy-done.2
  62.1 2.2 %shard_map.38 = f32[16,4,128]{2,1,0:T(4,128)} custom-call(f32[16,2,32,512]{3,2,1,0:T(8,128)S(1)} %all_to_all.40.refs_0_.x_ref, f32[2,8,512]{2,1,0:T(8,128)S(1)} %bitcast.1), custom_call_target="tpu_custom_call" | custom-call | flops 100663296 | bytes 1048576 | tf_op jit(solution)/shard_map/pallas_call | solution.py:270
  64.3 3.4 %all-to-all-start.1 = ((f32[16,4,128]{2,1,0:T(4,128)}), f32[16,4,128]{2,1,0:T(4,128)S(1)}, u32[]{:S(2)}, u32[]{:S(2)}) async-start(f32[16,4,128]{2,1,0:T(4,128)} %shard_map.38), calls=%async_computation.1 | async-start | bytes 65536 | tf_op jit(solution)/shard_map/all_to_all | solution.py:22
  67.7 0.0 copy-done.1
  67.7 1.8 shard_map.39.refs_0_
  69.5 5.1 %all-to-all-done.1 = f32[16,4,128]{2,1,0:T(4,128)S(1)} async-done(((f32[16,4,128]{2,1,0:T(4,128)}), f32[16,4,128]{2,1,0:T(4,128)S(1)}, u32[]{:S(2)}, u32[]{:S(2)}) %all-to-all-start.1) | async-done | bytes 32800 | tf_op jit(solution)/shard_map/all_to_all | solution.py:22
  74.7 20.6 %all_to_all.41 = f32[32,4,128]{2,1,0:T(4,128)S(1)} all-to-all(f32[32,4,128]{2,1,0:T(4,128)S(1)} %broadcast_in_dim.8), channel_id=1, replica_groups=mesh['chan'=16,'pix'=32] {'pix'}, dimensions={0} | all-to-all | bytes 131072 | tf_op jit(solution)/shard_map/all_to_all | solution.py:22
  95.3 11.7 %all_to_all.42.refs_1_ = f32[16,4,128]{2,1,0:T(4,128)S(1)} all-to-all(f32[16,4,128]{2,1,0:T(4,128)S(1)} %broadcast_in_dim.9), channel_id=1, replica_groups=mesh['chan'=16,'pix'=32] {'chan'}, dimensions={0} | all-to-all | bytes 65536 | tf_op jit(solution)/shard_map/all_to_all | solution.py:22
  107.0 2.4 %shard_map.40 = f32[16,4,128]{2,1,0:T(4,128)S(1)} custom-call(f32[16,2,32,512]{3,2,1,0:T(8,128)S(1)} %shard_map.39.refs_0_, f32[16,4,128]{2,1,0:T(4,128)S(1)} %all_to_all.42.refs_1_, bf16[3,2,256,256]{3,2,1,0:T(8,128)(2,1)S(1)} %copy-done.1), custom_call_target="tpu_custom_call" | custom-call | tf_op jit(solution)/shard_map/pallas_call | solution.py:286
  109.4 10.3 %all_to_all.43 = f32[16,4,128]{2,1,0:T(4,128)S(1)} all-to-all(f32[16,4,128]{2,1,0:T(4,128)S(1)} %shard_map.40), channel_id=1, replica_groups=mesh['chan'=16,'pix'=32] {'chan'}, dimensions={0} | all-to-all | bytes 65536 | tf_op jit(solution)/shard_map/all_to_all | solution.py:22
  119.7 11.9 %all_to_all.44 = f32[32,4,128]{2,1,0:T(4,128)S(1)} all-to-all(f32[32,4,128]{2,1,0:T(4,128)S(1)} %broadcast_in_dim.10), channel_id=1, replica_groups=mesh['chan'=16,'pix'=32] {'pix'}, dimensions={0} | all-to-all | bytes 131072 | tf_op jit(solution)/shard_map/all_to_all | solution.py:22
  131.6 11.5 %all_to_all.45.refs_1_ = f32[16,4,128]{2,1,0:T(4,128)S(1)} all-to-all(f32[16,4,128]{2,1,0:T(4,128)S(1)} %broadcast_in_dim.11), channel_id=1, replica_groups=mesh['chan'=16,'pix'=32] {'chan'}, dimensions={0} | all-to-all | bytes 65536 | tf_op jit(solution)/shard_map/all_to_all | solution.py:22
  143.1 1.7 shard_map.41
  144.9 53.9 %all_to_all.46.src = f32[16,2,4,32,128]{4,3,2,1,0:T(8,128)S(1)} all-to-all(f32[16,2,4,32,128]{4,3,2,1,0:T(8,128)S(1)} %shard_map.41), channel_id=1, replica_groups=mesh['chan'=16,'pix'=32] {'chan'}, dimensions={0} | all-to-all | bytes 4194304 | tf_op jit(solution)/shard_map/all_to_all | solution.py:22
  198.8 1.4 shard_map.42
  (8 shorter events, 0.2 us)
Async XLA Ops:
  0.0 1.6 copy-start
  1.7 60.4 %copy-start.2 = (f32[2,512,8]{1,2,0:T(8,128)S(1)}, f32[2,512,8]{1,2,0:T(8,128)}, u32[]{:S(2)}) copy-start(f32[2,512,8]{1,2,0:T(8,128)} %param.4) | copy-start | bytes 98308
  62.1 5.6 %copy-start.1 = (bf16[3,2,256,256]{3,2,1,0:T(8,128)(2,1)S(1)}, bf16[3,2,256,256]{3,2,1,0:T(8,128)(2,1)}, u32[]{:S(2)}) copy-start(bf16[3,2,256,256]{3,2,1,0:T(8,128)(2,1)} %constant.4.clone.table_ref.refs_2_) | copy-start | bytes 2359300
  64.3 10.3 %all-to-all-start.1 = ((f32[16,4,128]{2,1,0:T(4,128)}), f32[16,4,128]{2,1,0:T(4,128)S(1)}, u32[]{:S(2)}, u32[]{:S(2)}) async-start(f32[16,4,128]{2,1,0:T(4,128)} %shard_map.38), calls=%async_computation.1 | async-start | bytes 65536 | tf_op jit(solution)/shard_map/all_to_all | solution.py:22

commit v10 on v8

--- a/solution.py
+++ b/solution.py
@@ -222,13 +222,16 @@
     copies = []
     for h in range(halves):
         for s in range(species):
-            for j in range(src.shape[0]):
-                for c in range(src.shape[2]):
-                    at = (j * src.shape[2] + c) * LANES
-                    held[h, s, :, at : at + LANES] = src[j, s, c, h * waves : (h + 1) * waves]
-            copy = pltpu.make_async_copy(held.at[h, s], dst.at[h, s], sems.at[h, s])
-            copy.start()
-            copies.append(copy)
+            for r in range(waves // 8):
+                rows = pl.ds(r * 8, 8)
+                for j in range(src.shape[0]):
+                    for c in range(src.shape[2]):
+                        at = (j * src.shape[2] + c) * LANES
+                        first = h * waves + r * 8
+                        held[h, s, r * 8 : (r + 1) * 8, at : at + LANES] = src[j, s, c, first : first + 8]
+                copy = pltpu.make_async_copy(held.at[h, s, rows], dst.at[h, s, rows], sems.at[h, s, r])
+                copy.start()
+                copies.append(copy)
     for copy in copies:
         copy.wait()
 
@@ -299,7 +302,7 @@
     return pl.pallas_call(
         join_kernel,
         out_shape=shape(2, species, waves // owners, pixels), in_specs=[VMEM], out_specs=HBM, compiler_params=params(8),
-        scratch_shapes=[pltpu.VMEM((2, species, waves // owners, pixels), jnp.float32), DMA((2, species))],
+        scratch_shapes=[pltpu.VMEM((2, species, waves // owners, pixels), jnp.float32), DMA((2, species, waves // owners // 8))],
     )(swap(blocks, "chan"))
 
 

time: 201 us -> 201 us (level)
  no operation moved by 1% of the time
where the time goes in v10:
time: 201 us; the launch traced here: 200 us
  blocking collectives  180 us (90%)
  Pallas kernels  9.69 us (5%)
  waiting for transfers between devices  5.06 us (3%)
  starting transfers between devices  3.39 us (2%)
    all_to_all x7, blocking collectives, swap(): return lax.all_to_all(value, axis, split_axis=0, concat_axis=0, tiled=True)  180 us
    all_to_all x1, waiting for transfers between devices, swap(): return lax.all_to_all(value, axis, split_axis=0, concat_axis=0, tiled=True)  5.06 us
  transfers between devices with their start and end apart: 1, of which 1 were waited for; matrix products, arithmetic and copies ran while one was open for 0% of the time, Pallas kernels for 1%

profile of v10, /device:TPU:1, one launch (start us, length us, event | category | flops | bytes accessed | tf_op | source)
XLA Modules:
  0.0 200.2 jit_solution(401581530379843573)
XLA Ops:
  0.0 0.0 copy-start
  0.0 1.6 copy-done
  1.6 0.1 shard_map.37
  1.7 0.0 copy-start.2
  1.7 60.4 %all_to_all.40.refs_0_.x_ref = f32[16,2,32,512]{3,2,1,0:T(8,128)S(1)} all-to-all(f32[16,2,32,512]{3,2,1,0:T(8,128)S(1)} %shard_map.37), channel_id=1, replica_groups=mesh['chan'=16,'pix'=32] {'chan'}, dimensions={0} | all-to-all | bytes 4194304 | tf_op jit(solution)/shard_map/all_to_all | solution.py:22
  62.1 0.0 copy-start.1
  62.1 0.0 copy-done.2
  62.1 2.2 %shard_map.38 = f32[16,4,128]{2,1,0:T(4,128)} custom-call(f32[16,2,32,512]{3,2,1,0:T(8,128)S(1)} %all_to_all.40.refs_0_.x_ref, f32[2,8,512]{2,1,0:T(8,128)S(1)} %bitcast.1), custom_call_target="tpu_custom_call" | custom-call | flops 100663296 | bytes 1048576 | tf_op jit(solution)/shard_map/pallas_call | solution.py:274
  64.3 3.4 %all-to-all-start.1 = ((f32[16,4,128]{2,1,0:T(4,128)}), f32[16,4,128]{2,1,0:T(4,128)S(1)}, u32[]{:S(2)}, u32[]{:S(2)}) async-start(f32[16,4,128]{2,1,0:T(4,128)} %shard_map.38), calls=%async_computation.1 | async-start | bytes 65536 | tf_op jit(solution)/shard_map/all_to_all | solution.py:22
  67.7 0.0 copy-done.1
  67.7 1.8 shard_map.39.refs_0_
  69.5 5.1 %all-to-all-done.1 = f32[16,4,128]{2,1,0:T(4,128)S(1)} async-done(((f32[16,4,128]{2,1,0:T(4,128)}), f32[16,4,128]{2,1,0:T(4,128)S(1)}, u32[]{:S(2)}, u32[]{:S(2)}) %all-to-all-start.1) | async-done | bytes 32800 | tf_op jit(solution)/shard_map/all_to_all | solution.py:22
  74.7 20.6 %all_to_all.41 = f32[32,4,128]{2,1,0:T(4,128)S(1)} all-to-all(f32[32,4,128]{2,1,0:T(4,128)S(1)} %broadcast_in_dim.8), channel_id=1, replica_groups=mesh['chan'=16,'pix'=32] {'pix'}, dimensions={0} | all-to-all | bytes 131072 | tf_op jit(solution)/shard_map/all_to_all | solution.py:22
  95.3 11.7 %all_to_all.42.refs_1_ = f32[16,4,128]{2,1,0:T(4,128)S(1)} all-to-all(f32[16,4,128]{2,1,0:T(4,128)S(1)} %broadcast_in_dim.9), channel_id=1, replica_groups=mesh['chan'=16,'pix'=32] {'chan'}, dimensions={0} | all-to-all | bytes 65536 | tf_op jit(solution)/shard_map/all_to_all | solution.py:22
  107.0 2.4 %shard_map.40 = f32[16,4,128]{2,1,0:T(4,128)S(1)} custom-call(f32[16,2,32,512]{3,2,1,0:T(8,128)S(1)} %shard_map.39.refs_0_, f32[16,4,128]{2,1,0:T(4,128)S(1)} %all_to_all.42.refs_1_, bf16[3,2,256,256]{3,2,1,0:T(8,128)(2,1)S(1)} %copy-done.1), custom_call_target="tpu_custom_call" | custom-call | tf_op jit(solution)/shard_map/pallas_call | solution.py:290
  109.4 10.3 %all_to_all.43 = f32[16,4,128]{2,1,0:T(4,128)S(1)} all-to-all(f32[16,4,128]{2,1,0:T(4,128)S(1)} %shard_map.40), channel_id=1, replica_groups=mesh['chan'=16,'pix'=32] {'chan'}, dimensions={0} | all-to-all | bytes 65536 | tf_op jit(solution)/shard_map/all_to_all | solution.py:22
  119.7 11.9 %all_to_all.44 = f32[32,4,128]{2,1,0:T(4,128)S(1)} all-to-all(f32[32,4,128]{2,1,0:T(4,128)S(1)} %broadcast_in_dim.10), channel_id=1, replica_groups=mesh['chan'=16,'pix'=32] {'pix'}, dimensions={0} | all-to-all | bytes 131072 | tf_op jit(solution)/shard_map/all_to_all | solution.py:22
  131.6 11.5 %all_to_all.45.refs_1_ = f32[16,4,128]{2,1,0:T(4,128)S(1)} all-to-all(f32[16,4,128]{2,1,0:T(4,128)S(1)} %broadcast_in_dim.11), channel_id=1, replica_groups=mesh['chan'=16,'pix'=32] {'chan'}, dimensions={0} | all-to-all | bytes 65536 | tf_op jit(solution)/shard_map/all_to_all | solution.py:22
  143.1 1.8 shard_map.41
  144.9 53.9 %all_to_all.46.src = f32[16,2,4,32,128]{4,3,2,1,0:T(8,128)S(1)} all-to-all(f32[16,2,4,32,128]{4,3,2,1,0:T(8,128)S(1)} %shard_map.41), channel_id=1, replica_groups=mesh['chan'=16,'pix'=32] {'chan'}, dimensions={0} | all-to-all | bytes 4194304 | tf_op jit(solution)/shard_map/all_to_all | solution.py:22
  198.8 1.4 shard_map.42
  (8 shorter events, 0.2 us)
Async XLA Ops:
  0.0 1.6 copy-start
  1.7 60.4 %copy-start.2 = (f32[2,512,8]{1,2,0:T(8,128)S(1)}, f32[2,512,8]{1,2,0:T(8,128)}, u32[]{:S(2)}) copy-start(f32[2,512,8]{1,2,0:T(8,128)} %param.4) | copy-start | bytes 98308
  62.1 5.6 %copy-start.1 = (bf16[3,2,256,256]{3,2,1,0:T(8,128)(2,1)S(1)}, bf16[3,2,256,256]{3,2,1,0:T(8,128)(2,1)}, u32[]{:S(2)}) copy-start(bf16[3,2,256,256]{3,2,1,0:T(8,128)(2,1)} %constant.4.clone.table_ref.refs_2_) | copy-start | bytes 2359300
  64.3 10.3 %all-to-all-start.1 = ((f32[16,4,128]{2,1,0:T(4,128)}), f32[16,4,128]{2,1,0:T(4,128)S(1)}, u32[]{:S(2)}, u32[]{:S(2)}) async-start(f32[16,4,128]{2,1,0:T(4,128)} %shard_map.38), calls=%async_computation.1 | async-start | bytes 65536 | tf_op jit(solution)/shard_map/all_to_all | solution.py:22
